TPU v7x, 128 devices: a whole 4x4x4 slice. The times are simulated.
128 devices in a mesh: gx: 8 (over z, x_hi), gy: 4 (over x_lo, core), gz: 4 (over y).
Axes of the slice: x: 4 (x_hi: 2, x_lo: 2; x = x_hi * 2 + x_lo), y: 4, z: 4, core: 2. Of those that a mesh axis runs over, the one named last changes fastest.
Arguments:
- h_blocks: bfloat16 [8, 4, 4, 2, 48, 128, 128], P('gx', 'gy', 'gz'), may hold values from -0.0546875 to 0.0546875
- neighbours: int32 [8, 4, 4, 2, 48], P('gx', 'gy', 'gz'), may hold values from 0 to 53, as said below
- block_counts: int32 [8, 4, 4], P('gx', 'gy', 'gz'), may hold values from 1 to 2, as said below
- cheb_prev_in: bfloat16 [8, 4, 4, 2, 128, 128], P('gx', 'gy', 'gz'), may hold values from -6 to 6
- cheb_curr_in: bfloat16 [8, 4, 4, 2, 128, 128], P('gx', 'gy', 'gz'), may hold values from -6 to 6
- density_in: float32 [8, 4, 4, 2, 128, 128], P('gx', 'gy', 'gz'), may hold values from -6 to 6
- cheb_coeffs: float32 [2], replicated, may hold values from 0.2 to 1
Outputs:
- cheb_mid: bfloat16 [8, 4, 4, 2, 128, 128], P('gx', 'gy', 'gz')
- cheb_next: bfloat16 [8, 4, 4, 2, 128, 128], P('gx', 'gy', 'gz')
- density_out: float32 [8, 4, 4, 2, 128, 128], P('gx', 'gy', 'gz')
Inputs may be any that keep to these rules, and one draw needn't show every extreme that they name: `neighbours`: each row block lists 48 distinct entries. `block_counts`: cells in the first and last layers along the slab normal hold 1 block.
All inputs are finite; a program needn't handle non-finite values.
Results may differ from a plain program's by a relative error of at most 0.005.
Values may be sent and summed in bfloat16 or wider, within the bound.
A program may use at most 64 MiB of HBM per device.

v0:
```python
import jax
import jax.numpy as jnp
from jax import lax
from jax.sharding import PartitionSpec as P


def with_halo(block, sides, width):
    for axis, dim in sides:
        count = lax.axis_size(axis)
        forward = [(i, i + 1) for i in range(count - 1)]
        forward.append((count - 1, 0))
        backward = [(target, source) for source, target in forward]
        low = lax.ppermute(
            lax.slice_in_dim(block, block.shape[dim] - width, None, axis=dim), axis, forward
        )
        high = lax.ppermute(lax.slice_in_dim(block, 0, width, axis=dim), axis, backward)
        block = jnp.concatenate([low, block, high], axis=dim)
    return block


def on_device(
    h_blocks, neighbours, block_counts, cheb_prev_in, cheb_curr_in, density_in, cheb_coeffs
):
    slot_count = h_blocks.shape[3]
    coupled = h_blocks.shape[4]
    orbitals = h_blocks.shape[5]
    probes = cheb_prev_in.shape[5]
    slot_ids = jnp.arange(slot_count, dtype=jnp.int32)
    live_rows = (slot_ids[None, None, None, :] < block_counts[..., None]).astype(jnp.float32)[
        ..., None, None
    ]
    live_half = live_rows.astype(jnp.bfloat16)
    prev = cheb_prev_in * live_half
    curr = cheb_curr_in * live_half
    couplings = h_blocks.reshape(slot_count, coupled, orbitals, orbitals)
    picks_index = neighbours.reshape(-1)

    def hamiltonian_apply(vectors):
        padded = with_halo(vectors, (("gx", 0), ("gy", 1), ("gz", 2)), 1)
        candidates = padded.reshape(27 * slot_count, orbitals, probes)
        picked = jnp.take(candidates, picks_index, axis=0).reshape(
            slot_count, coupled, orbitals, probes
        )
        product = jnp.einsum(
            "rkab,rkbm->ram", couplings, picked, preferred_element_type=jnp.float32
        )
        return product.reshape(vectors.shape)

    cheb_mid = ((2.0 * hamiltonian_apply(curr) - prev.astype(jnp.float32)) * live_rows).astype(
        jnp.bfloat16
    )
    cheb_next = ((2.0 * hamiltonian_apply(cheb_mid) - curr.astype(jnp.float32)) * live_rows).astype(
        jnp.bfloat16
    )
    density_out = (
        density_in
        + cheb_coeffs[0] * cheb_mid.astype(jnp.float32)
        + cheb_coeffs[1] * cheb_next.astype(jnp.float32)
    )
    return (cheb_mid, cheb_next, density_out)


def solution(mesh):
    placed = (
        P("gx", "gy", "gz", None, None, None, None),
        P("gx", "gy", "gz", None, None),
        P("gx", "gy", "gz"),
        P("gx", "gy", "gz", None, None, None),
        P("gx", "gy", "gz", None, None, None),
        P("gx", "gy", "gz", None, None, None),
        P(),
    )
    return jax.shard_map(
        on_device,
        mesh=mesh,
        in_specs=placed,
        out_specs=(
            P("gx", "gy", "gz", None, None, None),
            P("gx", "gy", "gz", None, None, None),
            P("gx", "gy", "gz", None, None, None),
        ),
        check_vma=False,
    )
```

profile of v0, /device:TPU:1, one launch (start us, length us, event | category | flops | bytes accessed | tf_op | source)
XLA Modules:
  0.0 94.9 jit_solution(3477328983857399973)
XLA Ops:
  1.5 1.1 %copy.10 = bf16[1,1,1,2,128,128]{4,5,3,2,1,0:T(8,128)(2,1)S(1)} copy(bf16[1,1,1,2,128,128]{5,4,3,2,1,0:T(8,128)(2,1)} %param.13) | data formatting | bytes 131072 | tf_op args[4]
  2.6 3.6 %collective-permute-start = (bf16[1,1,1,2,128,128]{4,5,3,2,1,0:T(8,128)(2,1)S(1)}, bf16[1,1,1,2,128,128]{4,5,3,2,1,0:T(8,128)(2,1)S(1)}, u32[]{:S(2)}, u32[]{:S(2)}) collective-permute-start(bf16[1,1,1,2,128,128]{4,5,3,2,1,0:T(8,128)(2,1)S(1)} %broadcast_multiply_fusion), channel_id=1, source_target_pairs={{0,16},{16,32},{32,48},{48,64},{64,80},{80,96},{96,112},{112,0},{1... | collective-permute-start | bytes 196616 | tf_op jit(solution)/shard_map/ppermute | solution.py:13
  6.2 3.6 %collective-permute-start.1 = (bf16[1,1,1,2,128,128]{4,5,3,2,1,0:T(8,128)(2,1)S(1)}, bf16[1,1,1,2,128,128]{4,5,3,2,1,0:T(8,128)(2,1)S(1)}, u32[]{:S(2)}, u32[]{:S(2)}) collective-permute-start(bf16[1,1,1,2,128,128]{4,5,3,2,1,0:T(8,128)(2,1)S(1)} %broadcast_multiply_fusion), channel_id=1, source_target_pairs={{16,0},{32,16},{48,32},{64,48},{80,64},{96,80},{112,96},{0,112},{1... | collective-permute-start | bytes 196616 | tf_op jit(solution)/shard_map/ppermute | solution.py:16
  9.8 1.6 %collective-permute-done = bf16[1,1,1,2,128,128]{4,5,3,2,1,0:T(8,128)(2,1)S(1)} collective-permute-done((bf16[1,1,1,2,128,128]{4,5,3,2,1,0:T(8,128)(2,1)S(1)}, bf16[1,1,1,2,128,128]{4,5,3,2,1,0:T(8,128)(2,1)S(1)}, u32[]{:S(2)}, u32[]{:S(2)}) %collective-permute-start) | collective-permute-done | bytes 65568 | tf_op jit(solution)/shard_map/ppermute | solution.py:13
  11.6 1.8 %collective-permute-start.2 = (bf16[3,1,1,2,128,128]{4,5,3,2,1,0:T(8,128)(2,1)S(1)}, bf16[3,1,1,2,128,128]{4,5,3,2,1,0:T(8,128)(2,1)S(1)}, u32[]{:S(2)}, u32[]{:S(2)}) collective-permute-start(bf16[3,1,1,2,128,128]{4,5,3,2,1,0:T(8,128)(2,1)S(1)} %pad_maximum_fusion.4), channel_id=1, source_target_pairs={{0,4},{4,8},{8,12},{12,0},{1,5},{5,9},{9,13},{13,1},{2,6},{6,10},{... | collective-permute-start | bytes 589832 | tf_op jit(solution)/shard_map/ppermute | solution.py:13
  13.5 3.1 %collective-permute-done.2 = bf16[3,1,1,2,128,128]{4,5,3,2,1,0:T(8,128)(2,1)S(1)} collective-permute-done((bf16[3,1,1,2,128,128]{4,5,3,2,1,0:T(8,128)(2,1)S(1)}, bf16[3,1,1,2,128,128]{4,5,3,2,1,0:T(8,128)(2,1)S(1)}, u32[]{:S(2)}, u32[]{:S(2)}) %collective-permute-start.2) | collective-permute-done | bytes 196640 | tf_op jit(solution)/shard_map/ppermute | solution.py:13
  16.6 3.0 %collective-permute-done.3 = bf16[3,1,1,2,128,128]{4,5,3,2,1,0:T(8,128)(2,1)S(1)} collective-permute-done((bf16[3,1,1,2,128,128]{4,5,3,2,1,0:T(8,128)(2,1)S(1)}, bf16[3,1,1,2,128,128]{4,5,3,2,1,0:T(8,128)(2,1)S(1)}, u32[]{:S(2)}, u32[]{:S(2)}) %collective-permute-start.3) | collective-permute-done | bytes 196640 | tf_op jit(solution)/shard_map/ppermute | solution.py:16
  20.3 0.9 pad_maximum_fusion.2
  21.1 1.3 %collective-permute-start.4 = (bf16[3,3,1,2,128,128]{4,5,3,2,1,0:T(8,128)(2,1)}, bf16[3,3,1,2,128,128]{4,5,3,2,1,0:T(8,128)(2,1)}, u32[]{:S(2)}, u32[]{:S(2)}) collective-permute-start(bf16[3,3,1,2,128,128]{4,5,3,2,1,0:T(8,128)(2,1)} %pad_maximum_fusion.2), channel_id=1, source_target_pairs={{0,1},{1,2},{2,3},{3,0},{4,5},{5,6},{6,7},{7,4},{8,9},{9,10},{10,1... | collective-permute-start | bytes 1769480 | tf_op jit(solution)/shard_map/ppermute | solution.py:13
  22.4 1.4 %collective-permute-start.5 = (bf16[3,3,1,2,128,128]{4,5,3,2,1,0:T(8,128)(2,1)}, bf16[3,3,1,2,128,128]{4,5,3,2,1,0:T(8,128)(2,1)}, u32[]{:S(2)}, u32[]{:S(2)}) collective-permute-start(bf16[3,3,1,2,128,128]{4,5,3,2,1,0:T(8,128)(2,1)} %pad_maximum_fusion.2), channel_id=1, source_target_pairs={{1,0},{2,1},{3,2},{0,3},{5,4},{6,5},{7,6},{4,7},{9,8},{10,9},{11,1... | collective-permute-start | bytes 1769480 | tf_op jit(solution)/shard_map/ppermute | solution.py:16
  24.0 1.6 %copy.11 = bf16[1,1,1,2,128,128]{4,5,3,2,1,0:T(8,128)(2,1)} copy(bf16[1,1,1,2,128,128]{5,4,3,2,1,0:T(8,128)(2,1)} %param.12) | data formatting | bytes 131072 | tf_op args[3]
  26.2 11.8 %collective-permute-done.4 = bf16[3,3,1,2,128,128]{4,5,3,2,1,0:T(8,128)(2,1)} collective-permute-done((bf16[3,3,1,2,128,128]{4,5,3,2,1,0:T(8,128)(2,1)}, bf16[3,3,1,2,128,128]{4,5,3,2,1,0:T(8,128)(2,1)}, u32[]{:S(2)}, u32[]{:S(2)}) %collective-permute-start.4) | collective-permute-done | bytes 589856 | tf_op jit(solution)/shard_map/ppermute | solution.py:13
  38.1 2.5 %pad_maximum_fusion = bf16[3,3,3,2,128,128]{4,5,3,2,1,0:T(8,128)(2,1)} fusion(bf16[3,3,1,2,128,128]{4,5,3,2,1,0:T(8,128)(2,1)} %collective-permute-done.5, bf16[3,1,1,2,128,128]{4,5,3,2,1,0:T(8,128)(2,1)} %copy-done.1, bf16[1,1,1,2,128,128]{4,5,3,2,1,0:T(8,128)(2,1)S(1)} %collective-permute-done.1, ...), kind=kLoop, calls=%fused_computation.8 | loop fusion | flops 5308416 | bytes 3538944 | tf_op jit(solution)/shard_map/concatenate | solution.py:17
  40.5 4.2 %gather_fusion = bf16[96,128,128]{1,2,0:T(8,128)(2,1)} fusion(bf16[54,128,128]{1,2,0:T(8,128)(2,1)} %bitcast.89, s32[1024]{0:T(1024)S(1)} %pad_clamp_fusion), kind=kCustom, calls=%fused_computation.clone | custom fusion | bytes 6291840 | tf_op jit(solution)/shard_map/jit(_take)/gather | solution.py:41
  44.7 2.3 %broadcast_select_fusion.1 = bf16[96,128,128]{1,2,0:T(8,128)(2,1)S(1)} fusion(bf16[96,128,128]{1,2,0:T(8,128)(2,1)} %gather_fusion, pred[96]{0:T(512)(128)(4,1)S(1)} %compare_and_fusion), kind=kLoop, calls=%fused_computation.7 | loop fusion | flops 1572864 | bytes 6291552 | tf_op jit(solution)/shard_map/jit(_take)/select_n | solution.py:41
  47.0 1.0 %fusion.34 = bf16[1,1,1,2,128,128]{4,5,3,2,1,0:T(8,128)(2,1)S(1)} fusion(bf16[2,48,128,128]{2,3,1,0:T(8,128)(2,1)S(1)} %bitcast.91, bf16[1,1,1,2,48,128,128]{6,5,4,3,2,1,0:T(8,128)(2,1)S(1)} %copy-done, f32[2]{0:T(128)S(1)} %compare_convert_fusion, bf16[1,1,1,2,128,128]{4,5,3,2,1,0:T(8,128)(2,1)S(1)} %copy-done.5, bf16[2]{0:T(256)(128)(2,1)S(1)} %fusion.40), kind=kOutput, calls=%fused_computation.20 | convolution fusion | flops 402849792 | bytes 6422540 | tf_op jit(solution)/shard_map/rkab,rkbm->ram/dot_general | solution.py:44
  48.0 2.5 %collective-permute-start.6 = (bf16[1,1,1,2,128,128]{4,5,3,2,1,0:T(8,128)(2,1)S(1)}, bf16[1,1,1,2,128,128]{4,5,3,2,1,0:T(8,128)(2,1)S(1)}, u32[]{:S(2)}, u32[]{:S(2)}) collective-permute-start(bf16[1,1,1,2,128,128]{4,5,3,2,1,0:T(8,128)(2,1)S(1)} %fusion.34), channel_id=1, source_target_pairs={{0,16},{16,32},{32,48},{48,64},{64,80},{80,96},{96,112},{112,0},{1... | collective-permute-start | bytes 196616 | tf_op jit(solution)/shard_map/ppermute | solution.py:13
  50.5 2.9 %collective-permute-start.7 = (bf16[1,1,1,2,128,128]{4,5,3,2,1,0:T(8,128)(2,1)S(1)}, bf16[1,1,1,2,128,128]{4,5,3,2,1,0:T(8,128)(2,1)S(1)}, u32[]{:S(2)}, u32[]{:S(2)}) collective-permute-start(bf16[1,1,1,2,128,128]{4,5,3,2,1,0:T(8,128)(2,1)S(1)} %fusion.34), channel_id=1, source_target_pairs={{16,0},{32,16},{48,32},{64,48},{80,64},{96,80},{112,96},{0,112},{1... | collective-permute-start | bytes 196616 | tf_op jit(solution)/shard_map/ppermute | solution.py:16
  53.4 1.6 %collective-permute-done.6 = bf16[1,1,1,2,128,128]{4,5,3,2,1,0:T(8,128)(2,1)S(1)} collective-permute-done((bf16[1,1,1,2,128,128]{4,5,3,2,1,0:T(8,128)(2,1)S(1)}, bf16[1,1,1,2,128,128]{4,5,3,2,1,0:T(8,128)(2,1)S(1)}, u32[]{:S(2)}, u32[]{:S(2)}) %collective-permute-start.6) | collective-permute-done | bytes 65568 | tf_op jit(solution)/shard_map/ppermute | solution.py:13
  55.0 0.9 collective-permute-done.7
  56.0 2.3 %collective-permute-start.8 = (bf16[3,1,1,2,128,128]{4,5,3,2,1,0:T(8,128)(2,1)S(1)}, bf16[3,1,1,2,128,128]{4,5,3,2,1,0:T(8,128)(2,1)S(1)}, u32[]{:S(2)}, u32[]{:S(2)}) collective-permute-start(bf16[3,1,1,2,128,128]{4,5,3,2,1,0:T(8,128)(2,1)S(1)} %pad_maximum_fusion.5), channel_id=1, source_target_pairs={{0,4},{4,8},{8,12},{12,0},{1,5},{5,9},{9,13},{13,1},{2,6},{6,10},{... | collective-permute-start | bytes 589832 | tf_op jit(solution)/shard_map/ppermute | solution.py:13
  58.3 3.7 %collective-permute-done.8 = bf16[3,1,1,2,128,128]{4,5,3,2,1,0:T(8,128)(2,1)S(1)} collective-permute-done((bf16[3,1,1,2,128,128]{4,5,3,2,1,0:T(8,128)(2,1)S(1)}, bf16[3,1,1,2,128,128]{4,5,3,2,1,0:T(8,128)(2,1)S(1)}, u32[]{:S(2)}, u32[]{:S(2)}) %collective-permute-start.8) | collective-permute-done | bytes 196640 | tf_op jit(solution)/shard_map/ppermute | solution.py:13
  62.0 2.0 %collective-permute-done.9 = bf16[3,1,1,2,128,128]{4,5,3,2,1,0:T(8,128)(2,1)S(1)} collective-permute-done((bf16[3,1,1,2,128,128]{4,5,3,2,1,0:T(8,128)(2,1)S(1)}, bf16[3,1,1,2,128,128]{4,5,3,2,1,0:T(8,128)(2,1)S(1)}, u32[]{:S(2)}, u32[]{:S(2)}) %collective-permute-start.9) | collective-permute-done | bytes 196640 | tf_op jit(solution)/shard_map/ppermute | solution.py:16
  64.6 0.9 pad_maximum_fusion.3
  65.5 1.3 %collective-permute-start.10 = (bf16[3,3,1,2,128,128]{4,5,3,2,1,0:T(8,128)(2,1)}, bf16[3,3,1,2,128,128]{4,5,3,2,1,0:T(8,128)(2,1)}, u32[]{:S(2)}, u32[]{:S(2)}) collective-permute-start(bf16[3,3,1,2,128,128]{4,5,3,2,1,0:T(8,128)(2,1)} %pad_maximum_fusion.3), channel_id=1, source_target_pairs={{0,1},{1,2},{2,3},{3,0},{4,5},{5,6},{6,7},{7,4},{8,9},{9,10},{10,1... | collective-permute-start | bytes 1769480 | tf_op jit(solution)/shard_map/ppermute | solution.py:13
  66.8 1.4 %collective-permute-start.11 = (bf16[3,3,1,2,128,128]{4,5,3,2,1,0:T(8,128)(2,1)}, bf16[3,3,1,2,128,128]{4,5,3,2,1,0:T(8,128)(2,1)}, u32[]{:S(2)}, u32[]{:S(2)}) collective-permute-start(bf16[3,3,1,2,128,128]{4,5,3,2,1,0:T(8,128)(2,1)} %pad_maximum_fusion.3), channel_id=1, source_target_pairs={{1,0},{2,1},{3,2},{0,3},{5,4},{6,5},{7,6},{4,7},{9,8},{10,9},{11,1... | collective-permute-start | bytes 1769480 | tf_op jit(solution)/shard_map/ppermute | solution.py:16
  68.2 1.7 %copy.12 = f32[1,1,1,2,128,128]{4,5,3,2,1,0:T(8,128)} copy(f32[1,1,1,2,128,128]{5,4,3,2,1,0:T(8,128)} %param.14) | data formatting | bytes 262144 | tf_op args[5]
  71.2 11.1 %collective-permute-done.10 = bf16[3,3,1,2,128,128]{4,5,3,2,1,0:T(8,128)(2,1)} collective-permute-done((bf16[3,3,1,2,128,128]{4,5,3,2,1,0:T(8,128)(2,1)}, bf16[3,3,1,2,128,128]{4,5,3,2,1,0:T(8,128)(2,1)}, u32[]{:S(2)}, u32[]{:S(2)}) %collective-permute-start.10) | collective-permute-done | bytes 589856 | tf_op jit(solution)/shard_map/ppermute | solution.py:13
  82.3 2.5 %pad_maximum_fusion.1 = bf16[3,3,3,2,128,128]{4,5,3,2,1,0:T(8,128)(2,1)} fusion(bf16[3,3,1,2,128,128]{4,5,3,2,1,0:T(8,128)(2,1)} %collective-permute-done.11, bf16[3,1,1,2,128,128]{4,5,3,2,1,0:T(8,128)(2,1)} %copy-done.2, bf16[1,1,1,2,128,128]{4,5,3,2,1,0:T(8,128)(2,1)} %copy-done.3, bf16[1,1,1,2,128,128]{4,5,3,2,1,0:T(8,128)(2,1)S(1)} %fusion.34, ...), kind=kLoop, calls=%fused_computation.9 | loop fusion | flops 5308416 | bytes 3538944 | tf_op jit(solution)/shard_map/concatenate | solution.py:17
  84.8 4.2 %gather_fusion.1 = bf16[96,128,128]{1,2,0:T(8,128)(2,1)} fusion(bf16[54,128,128]{1,2,0:T(8,128)(2,1)} %bitcast.88, s32[1024]{0:T(1024)S(1)} %pad_clamp_fusion), kind=kCustom, calls=%fused_computation.1.clone | custom fusion | bytes 6291840 | tf_op jit(solution)/shard_map/jit(_take)/gather | solution.py:41
  88.9 2.3 %broadcast_select_fusion = bf16[96,128,128]{1,2,0:T(8,128)(2,1)S(1)} fusion(bf16[96,128,128]{1,2,0:T(8,128)(2,1)} %gather_fusion.1, pred[96]{0:T(512)(128)(4,1)S(1)} %compare_and_fusion), kind=kLoop, calls=%fused_computation.6 | loop fusion | flops 1572864 | bytes 6291552 | tf_op jit(solution)/shard_map/jit(_take)/select_n | solution.py:41
  91.2 2.2 %multiply_add_fusion = (f32[1,1,1,2,128,128]{4,5,3,2,1,0:T(8,128)S(1)}, bf16[1,1,1,2,128,128]{4,5,3,2,1,0:T(8,128)(2,1)S(1)}) fusion(f32[1,1,1,2,128,128]{4,5,3,2,1,0:T(8,128)S(1)} %copy-done.4, bf16[1,1,1,2,128,128]{4,5,3,2,1,0:T(8,128)(2,1)S(1)} %fusion.34, f32[]{:T(128)} %bitcast.15, f32[]{:T(128)} %bitcast.14, f32[2]{0:T(128)S(1)} %compare_convert_fusion, ...), kind=kOutput, calls=%fused_computation.26 | convolution fusion | flops 403013632 | bytes 6750224 | tf_op jit(solution)/shard_map/rkab,rkbm->ram/dot_general | solution.py:44
  (36 shorter events, 5.4 us)
Async XLA Ops:
  0.6 46.3 %copy-start = (bf16[1,1,1,2,48,128,128]{6,5,4,3,2,1,0:T(8,128)(2,1)S(1)}, bf16[1,1,1,2,48,128,128]{6,5,4,3,2,1,0:T(8,128)(2,1)}, u32[]{:S(2)}) copy-start(bf16[1,1,1,2,48,128,128]{6,5,4,3,2,1,0:T(8,128)(2,1)} %param.9) | copy-start | bytes 9437188
  0.6 23.2 %copy-start.7 = (s32[1,1,1,2,48]{4,3,2,1,0:T(2,128)S(1)}, s32[1,1,1,2,48]{4,3,2,1,0:T(2,128)}, u32[]{:S(2)}) copy-start(s32[1,1,1,2,48]{4,3,2,1,0:T(2,128)} %param.10) | copy-start | bytes 1156
  2.6 8.7 %collective-permute-start = (bf16[1,1,1,2,128,128]{4,5,3,2,1,0:T(8,128)(2,1)S(1)}, bf16[1,1,1,2,128,128]{4,5,3,2,1,0:T(8,128)(2,1)S(1)}, u32[]{:S(2)}, u32[]{:S(2)}) collective-permute-start(bf16[1,1,1,2,128,128]{4,5,3,2,1,0:T(8,128)(2,1)S(1)} %broadcast_multiply_fusion), channel_id=1, source_target_pairs={{0,16},{16,32},{32,48},{48,64},{64,80},{80,96},{96,112},{112,0},{1... | collective-permute-start | bytes 196616 | tf_op jit(solution)/shard_map/ppermute | solution.py:13
  6.2 5.4 %collective-permute-start.1 = (bf16[1,1,1,2,128,128]{4,5,3,2,1,0:T(8,128)(2,1)S(1)}, bf16[1,1,1,2,128,128]{4,5,3,2,1,0:T(8,128)(2,1)S(1)}, u32[]{:S(2)}, u32[]{:S(2)}) collective-permute-start(bf16[1,1,1,2,128,128]{4,5,3,2,1,0:T(8,128)(2,1)S(1)} %broadcast_multiply_fusion), channel_id=1, source_target_pairs={{16,0},{32,16},{48,32},{64,48},{80,64},{96,80},{112,96},{0,112},{1... | collective-permute-start | bytes 196616 | tf_op jit(solution)/shard_map/ppermute | solution.py:16
  11.6 5.0 %collective-permute-start.2 = (bf16[3,1,1,2,128,128]{4,5,3,2,1,0:T(8,128)(2,1)S(1)}, bf16[3,1,1,2,128,128]{4,5,3,2,1,0:T(8,128)(2,1)S(1)}, u32[]{:S(2)}, u32[]{:S(2)}) collective-permute-start(bf16[3,1,1,2,128,128]{4,5,3,2,1,0:T(8,128)(2,1)S(1)} %pad_maximum_fusion.4), channel_id=1, source_target_pairs={{0,4},{4,8},{8,12},{12,0},{1,5},{5,9},{9,13},{13,1},{2,6},{6,10},{... | collective-permute-start | bytes 589832 | tf_op jit(solution)/shard_map/ppermute | solution.py:13
  13.5 6.1 %collective-permute-start.3 = (bf16[3,1,1,2,128,128]{4,5,3,2,1,0:T(8,128)(2,1)S(1)}, bf16[3,1,1,2,128,128]{4,5,3,2,1,0:T(8,128)(2,1)S(1)}, u32[]{:S(2)}, u32[]{:S(2)}) collective-permute-start(bf16[3,1,1,2,128,128]{4,5,3,2,1,0:T(8,128)(2,1)S(1)} %pad_maximum_fusion.4), channel_id=1, source_target_pairs={{4,0},{8,4},{12,8},{0,12},{5,1},{9,5},{13,9},{1,13},{6,2},{10,6},{... | collective-permute-start | bytes 589832 | tf_op jit(solution)/shard_map/ppermute | solution.py:16
  19.6 0.7 copy-start.1
  21.1 16.9 %collective-permute-start.4 = (bf16[3,3,1,2,128,128]{4,5,3,2,1,0:T(8,128)(2,1)}, bf16[3,3,1,2,128,128]{4,5,3,2,1,0:T(8,128)(2,1)}, u32[]{:S(2)}, u32[]{:S(2)}) collective-permute-start(bf16[3,3,1,2,128,128]{4,5,3,2,1,0:T(8,128)(2,1)} %pad_maximum_fusion.2), channel_id=1, source_target_pairs={{0,1},{1,2},{2,3},{3,0},{4,5},{5,6},{6,7},{7,4},{8,9},{9,10},{10,1... | collective-permute-start | bytes 1769480 | tf_op jit(solution)/shard_map/ppermute | solution.py:13
  22.4 15.6 %collective-permute-start.5 = (bf16[3,3,1,2,128,128]{4,5,3,2,1,0:T(8,128)(2,1)}, bf16[3,3,1,2,128,128]{4,5,3,2,1,0:T(8,128)(2,1)}, u32[]{:S(2)}, u32[]{:S(2)}) collective-permute-start(bf16[3,3,1,2,128,128]{4,5,3,2,1,0:T(8,128)(2,1)} %pad_maximum_fusion.2), channel_id=1, source_target_pairs={{1,0},{2,1},{3,2},{0,3},{5,4},{6,5},{7,6},{4,7},{9,8},{10,9},{11,1... | collective-permute-start | bytes 1769480 | tf_op jit(solution)/shard_map/ppermute | solution.py:16
  24.0 1.6 %copy-start.8 = (s32[96]{0:T(128)}, s32[96]{0:T(128)S(1)}, u32[]{:S(2)}) copy-start(s32[96]{0:T(128)S(1)} %reshape.55) | copy-start | bytes 1156
  44.7 2.3 %copy-start.5 = (bf16[1,1,1,2,128,128]{4,5,3,2,1,0:T(8,128)(2,1)S(1)}, bf16[1,1,1,2,128,128]{4,5,3,2,1,0:T(8,128)(2,1)}, u32[]{:S(2)}) copy-start(bf16[1,1,1,2,128,128]{4,5,3,2,1,0:T(8,128)(2,1)} %copy.11) | copy-start | bytes 196612
  48.0 21.9 %copy-start.6 = (f32[2]{0:T(128)S(1)}, f32[2]{0:T(128)}, u32[]{:S(2)}) copy-start(f32[2]{0:T(128)} %param.15) | copy-start | bytes 28
  48.0 7.0 %collective-permute-start.6 = (bf16[1,1,1,2,128,128]{4,5,3,2,1,0:T(8,128)(2,1)S(1)}, bf16[1,1,1,2,128,128]{4,5,3,2,1,0:T(8,128)(2,1)S(1)}, u32[]{:S(2)}, u32[]{:S(2)}) collective-permute-start(bf16[1,1,1,2,128,128]{4,5,3,2,1,0:T(8,128)(2,1)S(1)} %fusion.34), channel_id=1, source_target_pairs={{0,16},{16,32},{32,48},{48,64},{64,80},{80,96},{96,112},{112,0},{1... | collective-permute-start | bytes 196616 | tf_op jit(solution)/shard_map/ppermute | solution.py:13
  50.5 5.4 %collective-permute-start.7 = (bf16[1,1,1,2,128,128]{4,5,3,2,1,0:T(8,128)(2,1)S(1)}, bf16[1,1,1,2,128,128]{4,5,3,2,1,0:T(8,128)(2,1)S(1)}, u32[]{:S(2)}, u32[]{:S(2)}) collective-permute-start(bf16[1,1,1,2,128,128]{4,5,3,2,1,0:T(8,128)(2,1)S(1)} %fusion.34), channel_id=1, source_target_pairs={{16,0},{32,16},{48,32},{64,48},{80,64},{96,80},{112,96},{0,112},{1... | collective-permute-start | bytes 196616 | tf_op jit(solution)/shard_map/ppermute | solution.py:16
  55.9 9.6 %copy-start.3 = (bf16[1,1,1,2,128,128]{4,5,3,2,1,0:T(8,128)(2,1)}, bf16[1,1,1,2,128,128]{4,5,3,2,1,0:T(8,128)(2,1)S(1)}, u32[]{:S(2)}) copy-start(bf16[1,1,1,2,128,128]{4,5,3,2,1,0:T(8,128)(2,1)S(1)} %collective-permute-done.7) | copy-start | bytes 196612
  56.0 6.0 %collective-permute-start.8 = (bf16[3,1,1,2,128,128]{4,5,3,2,1,0:T(8,128)(2,1)S(1)}, bf16[3,1,1,2,128,128]{4,5,3,2,1,0:T(8,128)(2,1)S(1)}, u32[]{:S(2)}, u32[]{:S(2)}) collective-permute-start(bf16[3,1,1,2,128,128]{4,5,3,2,1,0:T(8,128)(2,1)S(1)} %pad_maximum_fusion.5), channel_id=1, source_target_pairs={{0,4},{4,8},{8,12},{12,0},{1,5},{5,9},{9,13},{13,1},{2,6},{6,10},{... | collective-permute-start | bytes 589832 | tf_op jit(solution)/shard_map/ppermute | solution.py:13
  58.3 5.6 %collective-permute-start.9 = (bf16[3,1,1,2,128,128]{4,5,3,2,1,0:T(8,128)(2,1)S(1)}, bf16[3,1,1,2,128,128]{4,5,3,2,1,0:T(8,128)(2,1)S(1)}, u32[]{:S(2)}, u32[]{:S(2)}) collective-permute-start(bf16[3,1,1,2,128,128]{4,5,3,2,1,0:T(8,128)(2,1)S(1)} %pad_maximum_fusion.5), channel_id=1, source_target_pairs={{4,0},{8,4},{12,8},{0,12},{5,1},{9,5},{13,9},{1,13},{6,2},{10,6},{... | collective-permute-start | bytes 589832 | tf_op jit(solution)/shard_map/ppermute | solution.py:16
  63.9 0.7 copy-start.2
  65.5 16.8 %collective-permute-start.10 = (bf16[3,3,1,2,128,128]{4,5,3,2,1,0:T(8,128)(2,1)}, bf16[3,3,1,2,128,128]{4,5,3,2,1,0:T(8,128)(2,1)}, u32[]{:S(2)}, u32[]{:S(2)}) collective-permute-start(bf16[3,3,1,2,128,128]{4,5,3,2,1,0:T(8,128)(2,1)} %pad_maximum_fusion.3), channel_id=1, source_target_pairs={{0,1},{1,2},{2,3},{3,0},{4,5},{5,6},{6,7},{7,4},{8,9},{9,10},{10,1... | collective-permute-start | bytes 1769480 | tf_op jit(solution)/shard_map/ppermute | solution.py:13
  66.8 15.5 %collective-permute-start.11 = (bf16[3,3,1,2,128,128]{4,5,3,2,1,0:T(8,128)(2,1)}, bf16[3,3,1,2,128,128]{4,5,3,2,1,0:T(8,128)(2,1)}, u32[]{:S(2)}, u32[]{:S(2)}) collective-permute-start(bf16[3,3,1,2,128,128]{4,5,3,2,1,0:T(8,128)(2,1)} %pad_maximum_fusion.3), channel_id=1, source_target_pairs={{1,0},{2,1},{3,2},{0,3},{5,4},{6,5},{7,6},{4,7},{9,8},{10,9},{11,1... | collective-permute-start | bytes 1769480 | tf_op jit(solution)/shard_map/ppermute | solution.py:16
  88.9 2.3 %copy-start.4 = (f32[1,1,1,2,128,128]{4,5,3,2,1,0:T(8,128)S(1)}, f32[1,1,1,2,128,128]{4,5,3,2,1,0:T(8,128)}, u32[]{:S(2)}) copy-start(f32[1,1,1,2,128,128]{4,5,3,2,1,0:T(8,128)} %copy.12) | copy-start | bytes 393220
where the time goes:
time: 95.2 us; the launch traced here: 94.9 us
  waiting for transfers between devices  39 us (41%)
  starting transfers between devices  22.1 us (23%)
  local copies, waits for them, and re-layouts  17 us (18%)
  other arithmetic  12.1 us (13%)
  matrix products  3.14 us (3%)
  between operations  1.57 us (2%)
    ppermute x6, waiting for transfers between devices, with_halo(): lax.ppermute(lax.slice_in_dim(block, block.shape[dim] - width, None, axis...  32.8 us
    ppermute x6, starting transfers between devices, with_halo(): lax.ppermute(lax.slice_in_dim(block, block.shape[dim] - width, None, axis...  12.9 us
    ppermute x6, starting transfers between devices, with_halo(): lax.ppermute(lax.slice_in_dim(block, 0, width, axis=dim), axis, backward)  9.3 us
    gather x2, local copies, waits for them, and re-layouts, hamiltonian_apply(): jnp.take(candidates, picks_index, axis=0)  8.34 us
    unnamed x24, local copies, waits for them, and re-layouts  7.96 us
    concatenate x6, other arithmetic, with_halo(): block = jnp.concatenate([low, block, high], axis=dim)  6.78 us
    ppermute x6, waiting for transfers between devices, with_halo(): lax.ppermute(lax.slice_in_dim(block, 0, width, axis=dim), axis, backward)  6.12 us
    select_n x3, other arithmetic, hamiltonian_apply(): jnp.take(candidates, picks_index, axis=0)  4.54 us
  transfers between devices with their start and end apart: 12, of which 10 were waited for; matrix products, arithmetic and copies ran while one was open for 6% of the time, Pallas kernels for 0%

commit v1 on v0

v1 whole, which is shorter than its diff:
```python
import functools

import jax
import jax.numpy as jnp
from jax import lax
from jax.experimental import pallas as pl
from jax.experimental.pallas import tpu as pltpu
from jax.sharding import PartitionSpec as P

MESH = pl.DeviceIdType.MESH
OWN, CROSS, PARTNER = 0, 1, 2
ROUNDS = 2
SENDS = 64


def kernel(
    curr_hbm,
    prev_hbm,
    h_hbm,
    listed_hbm,
    counts_hbm,
    mid_ref,
    next_ref,
    first,
    second,
    blocks,
    prev,
    raw,
    total,
    place_rows,
    place,
    listed,
    counts,
    local_sem,
    send_sem,
    first_sem,
    second_sem,
):
    extent_x, extent_y, extent_z = (lax.axis_size(a) for a in ("gx", "gy", "gz"))
    x, y, z = (lax.axis_index(a) for a in ("gx", "gy", "gz"))
    slots, coupled = h_hbm.shape[3], h_hbm.shape[4]
    size = h_hbm.shape[5]
    side = 1 - 2 * (x % 2)
    near_x = (x + side + extent_x) % extent_x
    far_x = (x - side + extent_x) % extent_x
    lean = 1 - 2 * (y % 2)
    other_y = (y + lean + extent_y) % extent_y
    cross_y = (y - lean + extent_y) % extent_y
    up_z = (z + 1) % extent_z
    down_z = (z - 1 + extent_z) % extent_z

    other = (x, other_y, z)
    up, down = (x, y, up_z), (x, y, down_z)
    near, far = (near_x, y, z), (far_x, y, z)
    cross = ((x, cross_y, z), (near_x, cross_y, z), (far_x, cross_y, z))

    inner = (z > 0) & (z < extent_z - 1)
    toward = jnp.where(z < extent_z // 2, 1, -1)

    load_counts = pltpu.make_async_copy(counts_hbm, counts, local_sem.at[0])
    load_listed = pltpu.make_async_copy(listed_hbm, listed, local_sem.at[1])
    load_first = pltpu.make_async_copy(
        curr_hbm.at[0, 0, 0, 0], first.at[0, 0, OWN, 0], local_sem.at[2]
    )
    load_raw = pltpu.make_async_copy(curr_hbm.at[0, 0, 0, 1], raw, local_sem.at[3])
    load_blocks = pltpu.make_async_copy(
        h_hbm.at[0, 0, 0], blocks.at[:, pl.ds(0, coupled)], local_sem.at[4]
    )
    load_prev = pltpu.make_async_copy(prev_hbm.at[0, 0, 0], prev, local_sem.at[5])
    for load in (load_counts, load_listed, load_raw, load_first, load_blocks, load_prev):
        load.start()

    barrier = pltpu.get_barrier_semaphore()
    everyone = (near, far, *cross, up, down, other)
    for device in everyone:
        pl.semaphore_signal(barrier, inc=1, device_id=device, device_id_type=MESH)
    pl.semaphore_wait(barrier, len(everyone))

    pending = []

    def send(step, source, target, semaphore, device, when=None):
        index = len(pending)
        copy = pltpu.make_async_remote_copy(
            src_ref=source,
            dst_ref=target,
            send_sem=send_sem.at[index],
            recv_sem=semaphore,
            device_id=device,
            device_id_type=MESH,
        )
        pending.append((copy, when))
        if when is None:
            copy.start()
        else:
            pl.when(when)(copy.start)

    def arrived(buffer, semaphores, *index):
        ref = buffer.at[index]
        pltpu.make_async_remote_copy(
            src_ref=ref,
            dst_ref=ref,
            send_sem=send_sem.at[0],
            recv_sem=semaphores.at[index],
            device_id=other,
            device_id_type=MESH,
        ).wait_recv()

    def to_other(buffer, semaphores, *index, when=None):
        step, layer, column, group = index
        place_there = (step, layer, PARTNER, group)
        send(
            step,
            buffer.at[index],
            buffer.at[place_there],
            semaphores.at[place_there],
            other,
            when,
        )

    def along_z(step, source, column, group):
        for layer, device in ((1, up), (2, down)):
            at = (step, layer, column, group)
            send(step, source, first.at[at], first_sem.at[at], device)

    def along_xy(buffer, semaphores, step, layer, source, when=None):
        for column, group, device in (
            (OWN, 1, near),
            (OWN, 2, far),
            (CROSS, 1, cross[1]),
            (CROSS, 2, cross[2]),
            (CROSS, 0, cross[0]),
        ):
            at = (step, layer, column, group)
            send(step, source, buffer.at[at], semaphores.at[at], device, when)

    def send_first(step, source):
        along_xy(first, first_sem, step, 0, source)
        along_z(step, source, OWN, 0)
        at = (step, 0, PARTNER, 0)
        send(step, source, first.at[at], first_sem.at[at], other)

    def send_second(step):
        source = second.at[step, 0, OWN, 0]
        at = (step, 1, OWN, 0)
        send(step, source, second.at[at], second_sem.at[at], up, inner)
        send(step, source, second.at[at], second_sem.at[at], down, inner)
        along_xy(second, second_sem, step, 0, source, inner)
        to_other(second, second_sem, step, 0, OWN, 0, when=inner)

    shift_x = (0, side, -side)
    shift_y = (0, -lean, lean)

    def add(buffer, step, layer, column, slot, shift_z, start=False):
        rows = []
        for row in range(slots):
            parts = []
            for group in range(3):
                offset = (shift_x[group] + 1) * 9 + (shift_y[column] + 1) * 3 + shift_z + 1
                parts.append(blocks[row, place[row, offset * slots + slot]])
            rows.append(jnp.concatenate(parts, axis=1))
        product = jnp.dot(
            jnp.concatenate(rows, axis=0),
            buffer[step, layer, column].reshape(3 * size, -1),
            preferred_element_type=jnp.float32,
        )
        if start:
            total[...] = product
        else:
            total[...] += product

    def apply(step, before_blocks):
        arrived(first, first_sem, step, 0, OWN, 1)
        along_z(step, first.at[step, 0, OWN, 1], OWN, 1)
        arrived(second, second_sem, step, 1, OWN, 0)
        along_xy(second, second_sem, step, 1, second.at[step, 1, OWN, 0])
        arrived(first, first_sem, step, 0, OWN, 2)
        along_z(step, first.at[step, 0, OWN, 2], OWN, 2)
        for group in (1, 2, 0):
            arrived(first, first_sem, step, 0, CROSS, group)
            along_z(step, first.at[step, 0, CROSS, group], CROSS, group)
        for group in (1, 2):
            to_other(first, first_sem, step, 0, OWN, group)
        to_other(second, second_sem, step, 1, OWN, 0)

        before_blocks()
        add(first, step, 0, OWN, 0, 0, start=True)
        for layer in (1, 2):
            arrived(first, first_sem, step, layer, OWN, 0)
            to_other(first, first_sem, step, layer, OWN, 0)
        add(first, step, 0, CROSS, 0, 0)

        @pl.when(inner)
        def _():
            for group in (1, 2):
                arrived(second, second_sem, step, 0, OWN, group)

        for group in (1, 2):
            to_other(second, second_sem, step, 0, OWN, group, when=inner)
        for layer in (1, 2):
            arrived(first, first_sem, step, layer, OWN, 1)
            to_other(first, first_sem, step, layer, OWN, 1)

        @pl.when(inner)
        def _():
            for group in (0, 1, 2):
                arrived(second, second_sem, step, 0, CROSS, group)
            add(second, step, 0, OWN, 1, 0)
            add(second, step, 0, CROSS, 1, 0)

        for group in (0, 1, 2):
            arrived(first, first_sem, step, 0, PARTNER, group)
        add(first, step, 0, PARTNER, 0, 0)

        for layer in (1, 2):
            arrived(first, first_sem, step, layer, OWN, 2)
            to_other(first, first_sem, step, layer, OWN, 2)
        for group in (1, 2):
            arrived(second, second_sem, step, 1, OWN, group)
            to_other(second, second_sem, step, 1, OWN, group)

        @pl.when(inner)
        def _():
            for group in (0, 1, 2):
                arrived(second, second_sem, step, 0, PARTNER, group)
            add(second, step, 0, PARTNER, 1, 0)

        add(second, step, 1, OWN, 1, toward)
        for layer in (1, 2):
            shift = -1 if layer == 1 else 1
            add(first, step, layer, OWN, 0, shift)
        for layer in (1, 2):
            shift = -1 if layer == 1 else 1
            for group in (0, 1, 2):
                arrived(first, first_sem, step, layer, CROSS, group)
            add(first, step, layer, CROSS, 0, shift)
            for group in (0, 1, 2):
                arrived(first, first_sem, step, layer, PARTNER, group)
            add(first, step, layer, PARTNER, 0, shift)
        for group in (0, 1, 2):
            arrived(second, second_sem, step, 1, CROSS, group)
        add(second, step, 1, CROSS, 1, toward)
        for group in (0, 1, 2):
            arrived(second, second_sem, step, 1, PARTNER, group)
        add(second, step, 1, PARTNER, 1, toward)

    def settle():
        for copy, when in pending:
            if when is None:
                copy.wait_send()
            else:
                pl.when(when)(copy.wait_send)

    send_first(0, curr_hbm.at[0, 0, 0, 0])
    load_counts.wait()
    load_raw.wait()
    live = counts[0, 0, 0] > 1
    second[0, 0, OWN, 0] = jnp.where(live, raw[...].astype(jnp.float32), 0.0).astype(raw.dtype)
    send_second(0)

    load_listed.wait()
    blocks[:, pl.ds(coupled, 1)] = jnp.zeros((slots, 1, size, size), blocks.dtype)
    lanes = lax.broadcasted_iota(jnp.int32, (1, place_rows.shape[1]), 1)
    for row in range(slots):
        found = jnp.full(lanes.shape, coupled, jnp.int32)
        for item in range(coupled):
            found = jnp.where(lanes == listed[0, 0, 0, row, item], item, found)
        place_rows[pl.ds(row, 1), :] = found
    load_place = pltpu.make_async_copy(place_rows, place, local_sem.at[6])
    load_place.start()
    load_first.wait()
    load_prev.wait()

    def ready():
        load_place.wait()
        load_blocks.wait()

    apply(0, ready)

    def mid_of(row):
        return 2.0 * total[pl.ds(row * size, size), :] - prev[row].astype(jnp.float32)

    mid = mid_of(0).astype(raw.dtype)
    first[1, 0, OWN, 0] = mid
    send_first(1, first.at[1, 0, OWN, 0])
    mid_ref[0, 0, 0, 0] = mid
    mid = jnp.where(live, mid_of(1), 0.0).astype(raw.dtype)
    second[1, 0, OWN, 0] = mid
    send_second(1)
    mid_ref[0, 0, 0, 1] = mid

    apply(1, lambda: None)
    next_ref[0, 0, 0, 0] = (
        2.0 * total[pl.ds(0, size), :] - first[0, 0, OWN, 0].astype(jnp.float32)
    ).astype(raw.dtype)
    next_ref[0, 0, 0, 1] = jnp.where(
        live,
        2.0 * total[pl.ds(size, size), :] - second[0, 0, OWN, 0].astype(jnp.float32),
        0.0,
    ).astype(raw.dtype)
    settle()


def on_device(
    h_blocks, neighbours, block_counts, cheb_prev_in, cheb_curr_in, density_in, cheb_coeffs
):
    slots, coupled, size = h_blocks.shape[3:6]
    field = cheb_curr_in.shape
    probes = field[5]
    kind = cheb_curr_in.dtype
    anywhere = pl.BlockSpec(memory_space=pl.ANY)
    in_vmem = pl.BlockSpec(memory_space=pltpu.VMEM)
    cheb_mid, cheb_next = pl.pallas_call(
        kernel,
        name="two_steps",
        out_shape=(jax.ShapeDtypeStruct(field, kind), jax.ShapeDtypeStruct(field, kind)),
        in_specs=[anywhere] * 5,
        out_specs=(in_vmem, in_vmem),
        scratch_shapes=[
            pltpu.VMEM((ROUNDS, 3, 3, 3, size, probes), kind),
            pltpu.VMEM((ROUNDS, 2, 3, 3, size, probes), kind),
            pltpu.VMEM((slots, coupled + 1, size, size), h_blocks.dtype),
            pltpu.VMEM((slots, size, probes), kind),
            pltpu.VMEM((size, probes), kind),
            pltpu.VMEM((slots * size, probes), jnp.float32),
            pltpu.VMEM((8, 128), jnp.int32),
            pltpu.SMEM((8, 128), jnp.int32),
            pltpu.SMEM(neighbours.shape, jnp.int32),
            pltpu.SMEM(block_counts.shape, jnp.int32),
            pltpu.SemaphoreType.DMA((8,)),
            pltpu.SemaphoreType.DMA((ROUNDS * SENDS,)),
            pltpu.SemaphoreType.DMA((ROUNDS, 3, 3, 3)),
            pltpu.SemaphoreType.DMA((ROUNDS, 2, 3, 3)),
        ],
        compiler_params=pltpu.CompilerParams(
            collective_id=0, has_side_effects=True, vmem_limit_bytes=32 * 2**20
        ),
    )(cheb_curr_in, cheb_prev_in, h_blocks, neighbours, block_counts)
    density_out = (
        density_in
        + cheb_coeffs[0] * cheb_mid.astype(jnp.float32)
        + cheb_coeffs[1] * cheb_next.astype(jnp.float32)
    )
    return (cheb_mid, cheb_next, density_out)


def solution(mesh):
    placed = (
        P("gx", "gy", "gz", None, None, None, None),
        P("gx", "gy", "gz", None, None),
        P("gx", "gy", "gz"),
        P("gx", "gy", "gz", None, None, None),
        P("gx", "gy", "gz", None, None, None),
        P("gx", "gy", "gz", None, None, None),
        P(),
    )
    return jax.shard_map(
        on_device,
        mesh=mesh,
        in_specs=placed,
        out_specs=(
            P("gx", "gy", "gz", None, None, None),
            P("gx", "gy", "gz", None, None, None),
            P("gx", "gy", "gz", None, None, None),
        ),
        check_vma=False,
    )
```

time: 95.2 us -> 45.3 us (0.48)
  waiting for transfers between devices: 39 us -> 0 us
  Pallas kernels: 0 us -> 35.6 us
  starting transfers between devices: 22.1 us -> 0 us
  local copies, waits for them, and re-layouts: 17 us -> 6.09 us
  other arithmetic: 12.1 us -> 1.98 us
  matrix products: 3.14 us -> 0 us
    ppermute x12 -> x0, waiting for transfers between devices: 39 us -> none  [the longest x6 32.8 us: with_halo(): lax.ppermute(lax.slice_in_dim(block, block.shape[dim] - width, None, axis...]
    pallas_call x0 -> x1, Pallas kernels: none -> 35.6 us  [on_device(): pl.pallas_call(kernel, name='two_steps', out_shape=(jax.ShapeDtypeStruct(...]
    ppermute x12 -> x0, starting transfers between devices: 22.1 us -> none  [the longest x6 12.9 us: with_halo(): lax.ppermute(lax.slice_in_dim(block, block.shape[dim] - width, None, axis...]
    gather x2 -> x0, local copies, waits for them, and re-layouts: 8.34 us -> none  [hamiltonian_apply(): jnp.take(candidates, picks_index, axis=0)]
    concatenate x6 -> x0, other arithmetic: 6.78 us -> none  [with_halo(): block = jnp.concatenate([low, block, high], axis=dim)]
    select_n x3 -> x0, other arithmetic: 4.54 us -> none  [hamiltonian_apply(): jnp.take(candidates, picks_index, axis=0)]
    dot_general x2 -> x0, matrix products: 3.14 us -> none  [hamiltonian_apply(): jnp.einsum('rkab,rkbm->ram', couplings, picked, preferred_element_type=jn...]
    unnamed x24 -> x14, local copies, waits for them, and re-layouts: 7.96 us -> 5.5 us
  transfers between devices with their start and end apart: 12 -> 0, of which waited for: 10 -> 0; matrix products, arithmetic and copies ran while one was open for 6% -> 0% of each run, Pallas kernels for 0% -> 0%
where the time goes in v1:
time: 45.3 us; the launch traced here: 45 us
  Pallas kernels  35.6 us (79%)
  local copies, waits for them, and re-layouts  6.09 us (13%)
  other arithmetic  1.98 us (4%)
  between operations  1.33 us (3%)
    pallas_call x1, Pallas kernels, on_device(): pl.pallas_call(kernel, name='two_steps', out_shape=(jax.ShapeDtypeStruct(...  35.6 us
    unnamed x14, local copies, waits for them, and re-layouts  5.5 us
    add x1, other arithmetic, on_device(): density_in + cheb_coeffs[0] * cheb_mid.astype(jnp.float32)  1.98 us

profile of v1, /device:TPU:1, one launch (start us, length us, event | category | flops | bytes accessed | tf_op | source)
XLA Modules:
  0.0 45.0 jit_solution(16810387805040032927)
XLA Ops:
  0.6 0.0 copy-start.5
  1.3 0.0 copy-start
  1.3 1.9 %copy-done = bf16[1,1,1,2,48,128,128]{6,5,4,3,2,1,0:T(8,128)(2,1)S(1)} copy-done((bf16[1,1,1,2,48,128,128]{6,5,4,3,2,1,0:T(8,128)(2,1)S(1)}, bf16[1,1,1,2,48,128,128]{6,5,4,3,2,1,0:T(8,128)(2,1)}, u32[]{:S(2)}) %copy-start) | copy-done | bytes 3145752
  3.2 0.0 copy-start.1
  3.2 0.8 %copy-done.1 = bf16[1,1,1,2,128,128]{5,4,3,2,1,0:T(8,128)(2,1)S(1)} copy-done((bf16[1,1,1,2,128,128]{5,4,3,2,1,0:T(8,128)(2,1)S(1)}, bf16[1,1,1,2,128,128]{5,4,3,2,1,0:T(8,128)(2,1)}, u32[]{:S(2)}) %copy-start.1) | copy-done | bytes 65560
  4.0 0.0 copy-start.2
  4.0 0.8 %copy-done.2 = bf16[1,1,1,2,128,128]{5,4,3,2,1,0:T(8,128)(2,1)S(1)} copy-done((bf16[1,1,1,2,128,128]{5,4,3,2,1,0:T(8,128)(2,1)S(1)}, bf16[1,1,1,2,128,128]{5,4,3,2,1,0:T(8,128)(2,1)}, u32[]{:S(2)}) %copy-start.2) | copy-done | bytes 65560
  4.9 0.0 copy-start.3
  4.9 0.7 %copy-done.3 = s32[1,1,1,2,48]{4,3,2,1,0:T(2,128)S(1)} copy-done((s32[1,1,1,2,48]{4,3,2,1,0:T(2,128)S(1)}, s32[1,1,1,2,48]{4,3,2,1,0:T(2,128)}, u32[]{:S(2)}) %copy-start.3) | copy-done | bytes 408
  5.6 0.0 copy-start.4
  5.6 35.6 %two_steps.1 = (bf16[1,1,1,2,128,128]{5,4,3,2,1,0:T(8,128)(2,1)S(1)}, bf16[1,1,1,2,128,128]{5,4,3,2,1,0:T(8,128)(2,1)S(1)}) custom-call(bf16[1,1,1,2,128,128]{5,4,3,2,1,0:T(8,128)(2,1)S(1)} %copy-done.1, bf16[1,1,1,2,128,128]{5,4,3,2,1,0:T(8,128)(2,1)S(1)} %copy-done.2, bf16[1,1,1,2,48,128,128]{6,5,4,3,2,1,0:T(8,128)(2,1)S(1)} %copy-done, ...), custom_call_target="tpu_custom_call" | custom-call | tf_op jit(solution)/shard_map/two_steps/pallas_call | solution.py:312
  41.2 0.0 copy-done.5
  41.2 0.6 %fusion = (f32[1]{0:T(128)}, f32[1]{0:T(128)}) fusion(f32[2]{0:T(128)S(1)} %copy-done.5), kind=kLoop, calls=%fused_computation.1 | loop fusion | bytes 16 | tf_op jit(solution)/shard_map/slice | solution.py:340
  41.8 0.0 copy-done.4
  41.8 2.0 %multiply_add_fusion = f32[1,1,1,2,128,128]{5,4,3,2,1,0:T(8,128)} fusion(bf16[1,1,1,2,128,128]{5,4,3,2,1,0:T(8,128)(2,1)S(1)} %get-tuple-element.13, f32[1,1,1,2,128,128]{5,4,3,2,1,0:T(8,128)S(1)} %copy-done.4, bf16[1,1,1,2,128,128]{5,4,3,2,1,0:T(8,128)(2,1)S(1)} %get-tuple-element.12, f32[]{:T(128)} %bitcast.1, f32[]{:T(128)} %bitcast), kind=kLoop, calls=%fused_computation | loop fusion | flops 196608 | bytes 393224 | tf_op jit(solution)/shard_map/add | solution.py:339
  43.8 0.6 %copy.13 = bf16[1,1,1,2,128,128]{5,4,3,2,1,0:T(8,128)(2,1)} copy(bf16[1,1,1,2,128,128]{5,4,3,2,1,0:T(8,128)(2,1)S(1)} %get-tuple-element.12) | data formatting | bytes 131072
  44.4 0.6 %copy.14 = bf16[1,1,1,2,128,128]{5,4,3,2,1,0:T(8,128)(2,1)} copy(bf16[1,1,1,2,128,128]{5,4,3,2,1,0:T(8,128)(2,1)S(1)} %get-tuple-element.13) | data formatting | bytes 131072
Async XLA Ops:
  0.6 40.6 %copy-start.5 = (f32[2]{0:T(128)S(1)}, f32[2]{0:T(128)}, u32[]{:S(2)}) copy-start(f32[2]{0:T(128)} %param.13) | copy-start | bytes 28
  1.3 1.9 %copy-start = (bf16[1,1,1,2,48,128,128]{6,5,4,3,2,1,0:T(8,128)(2,1)S(1)}, bf16[1,1,1,2,48,128,128]{6,5,4,3,2,1,0:T(8,128)(2,1)}, u32[]{:S(2)}) copy-start(bf16[1,1,1,2,48,128,128]{6,5,4,3,2,1,0:T(8,128)(2,1)} %h_hbm.1) | copy-start | bytes 9437188
  3.2 0.8 %copy-start.1 = (bf16[1,1,1,2,128,128]{5,4,3,2,1,0:T(8,128)(2,1)S(1)}, bf16[1,1,1,2,128,128]{5,4,3,2,1,0:T(8,128)(2,1)}, u32[]{:S(2)}) copy-start(bf16[1,1,1,2,128,128]{5,4,3,2,1,0:T(8,128)(2,1)} %curr_hbm.1) | copy-start | bytes 196612
  4.0 0.8 %copy-start.2 = (bf16[1,1,1,2,128,128]{5,4,3,2,1,0:T(8,128)(2,1)S(1)}, bf16[1,1,1,2,128,128]{5,4,3,2,1,0:T(8,128)(2,1)}, u32[]{:S(2)}) copy-start(bf16[1,1,1,2,128,128]{5,4,3,2,1,0:T(8,128)(2,1)} %prev_hbm.1) | copy-start | bytes 196612
  4.9 0.7 %copy-start.3 = (s32[1,1,1,2,48]{4,3,2,1,0:T(2,128)S(1)}, s32[1,1,1,2,48]{4,3,2,1,0:T(2,128)}, u32[]{:S(2)}) copy-start(s32[1,1,1,2,48]{4,3,2,1,0:T(2,128)} %listed_hbm.1) | copy-start | bytes 1156
  5.6 36.3 %copy-start.4 = (f32[1,1,1,2,128,128]{5,4,3,2,1,0:T(8,128)S(1)}, f32[1,1,1,2,128,128]{5,4,3,2,1,0:T(8,128)}, u32[]{:S(2)}) copy-start(f32[1,1,1,2,128,128]{5,4,3,2,1,0:T(8,128)} %param.12) | copy-start | bytes 393220

commit v2 on v1

--- a/solution.py
+++ b/solution.py
@@ -19,8 +19,11 @@
     h_hbm,
     listed_hbm,
     counts_hbm,
+    density_hbm,
+    coeffs_hbm,
     mid_ref,
     next_ref,
+    density_ref,
     first,
     second,
     blocks,
@@ -31,6 +34,7 @@
     place,
     listed,
     counts,
+    coeffs,
     local_sem,
     send_sem,
     first_sem,
@@ -67,7 +71,18 @@
         h_hbm.at[0, 0, 0], blocks.at[:, pl.ds(0, coupled)], local_sem.at[4]
     )
     load_prev = pltpu.make_async_copy(prev_hbm.at[0, 0, 0], prev, local_sem.at[5])
-    for load in (load_counts, load_listed, load_raw, load_first, load_blocks, load_prev):
+    load_density = pltpu.make_async_copy(density_hbm, density_ref, local_sem.at[7])
+    load_coeffs = pltpu.make_async_copy(coeffs_hbm, coeffs, local_sem.at[8])
+    for load in (
+        load_counts,
+        load_listed,
+        load_raw,
+        load_first,
+        load_blocks,
+        load_prev,
+        load_density,
+        load_coeffs,
+    ):
         load.start()
 
     barrier = pltpu.get_barrier_semaphore()
@@ -288,16 +303,31 @@
     send_second(1)
     mid_ref[0, 0, 0, 1] = mid
 
+    load_density.wait()
+    load_coeffs.wait()
+    density_ref[...] += coeffs[0] * mid_ref[...].astype(jnp.float32)
     apply(1, lambda: None)
-    next_ref[0, 0, 0, 0] = (
-        2.0 * total[pl.ds(0, size), :] - first[0, 0, OWN, 0].astype(jnp.float32)
-    ).astype(raw.dtype)
-    next_ref[0, 0, 0, 1] = jnp.where(
-        live,
-        2.0 * total[pl.ds(size, size), :] - second[0, 0, OWN, 0].astype(jnp.float32),
-        0.0,
-    ).astype(raw.dtype)
+    for row, held in ((0, first), (1, second)):
+        value = 2.0 * total[pl.ds(row * size, size), :] - held[0, 0, OWN, 0].astype(jnp.float32)
+        if row:
+            value = jnp.where(live, value, 0.0)
+        value = value.astype(raw.dtype)
+        next_ref[0, 0, 0, row] = value
+        density_ref[0, 0, 0, row] += coeffs[1] * value.astype(jnp.float32)
     settle()
+
+
+def hand_over(*refs):
+    count = len(refs) // 2
+    sources, targets, semaphores = refs[:count], refs[count : 2 * count], refs[-1]
+    copies = [
+        pltpu.make_async_copy(source, target, semaphores.at[index])
+        for index, (source, target) in enumerate(zip(sources, targets))
+    ]
+    for copy in copies:
+        copy.start()
+    for copy in copies:
+        copy.wait()
 
 
 def on_device(
@@ -307,14 +337,20 @@
     field = cheb_curr_in.shape
     probes = field[5]
     kind = cheb_curr_in.dtype
-    anywhere = pl.BlockSpec(memory_space=pl.ANY)
+    in_hbm = pl.BlockSpec(memory_space=pltpu.HBM)
+    kept = functools.partial(pltpu.with_memory_space_constraint, memory_space=pltpu.HBM)
     in_vmem = pl.BlockSpec(memory_space=pltpu.VMEM)
-    cheb_mid, cheb_next = pl.pallas_call(
+    results = (
+        jax.ShapeDtypeStruct(field, kind),
+        jax.ShapeDtypeStruct(field, kind),
+        jax.ShapeDtypeStruct(field, jnp.float32),
+    )
+    made = pl.pallas_call(
         kernel,
         name="two_steps",
-        out_shape=(jax.ShapeDtypeStruct(field, kind), jax.ShapeDtypeStruct(field, kind)),
-        in_specs=[anywhere] * 5,
-        out_specs=(in_vmem, in_vmem),
+        out_shape=results,
+        in_specs=[in_hbm] * 7,
+        out_specs=(in_vmem,) * 3,
         scratch_shapes=[
             pltpu.VMEM((ROUNDS, 3, 3, 3, size, probes), kind),
             pltpu.VMEM((ROUNDS, 2, 3, 3, size, probes), kind),
@@ -326,7 +362,8 @@
             pltpu.SMEM((8, 128), jnp.int32),
             pltpu.SMEM(neighbours.shape, jnp.int32),
             pltpu.SMEM(block_counts.shape, jnp.int32),
-            pltpu.SemaphoreType.DMA((8,)),
+            pltpu.SMEM(cheb_coeffs.shape, jnp.float32),
+            pltpu.SemaphoreType.DMA((9,)),
             pltpu.SemaphoreType.DMA((ROUNDS * SENDS,)),
             pltpu.SemaphoreType.DMA((ROUNDS, 3, 3, 3)),
             pltpu.SemaphoreType.DMA((ROUNDS, 2, 3, 3)),
@@ -334,13 +371,25 @@
         compiler_params=pltpu.CompilerParams(
             collective_id=0, has_side_effects=True, vmem_limit_bytes=32 * 2**20
         ),
-    )(cheb_curr_in, cheb_prev_in, h_blocks, neighbours, block_counts)
-    density_out = (
-        density_in
-        + cheb_coeffs[0] * cheb_mid.astype(jnp.float32)
-        + cheb_coeffs[1] * cheb_next.astype(jnp.float32)
-    )
-    return (cheb_mid, cheb_next, density_out)
+    )(
+        kept(cheb_curr_in),
+        kept(cheb_prev_in),
+        kept(h_blocks),
+        kept(neighbours),
+        block_counts,
+        kept(density_in),
+        kept(cheb_coeffs),
+    )
+    return tuple(
+        pl.pallas_call(
+            hand_over,
+            name="hand_over",
+            out_shape=results,
+            in_specs=[pl.BlockSpec(memory_space=pl.ANY)] * 3,
+            out_specs=(in_hbm,) * 3,
+            scratch_shapes=[pltpu.SemaphoreType.DMA((3,))],
+        )(*made)
+    )
 
 
 def solution(mesh):

time: 45.3 us -> 48.3 us (1.066)
  Pallas kernels: 35.6 us -> 45 us
  local copies, waits for them, and re-layouts: 6.09 us -> 1.87 us
  other arithmetic: 1.98 us -> 0 us
    pallas_call x1 -> x2, Pallas kernels: 35.6 us -> 45 us  [the longest x1 35.9 us: on_device(): pl.pallas_call(kernel, name='two_steps', out_shape=results, in_specs=[in_...]
    unnamed x14 -> x6, local copies, waits for them, and re-layouts: 5.5 us -> 1.87 us
    add x1 -> x0, other arithmetic: 1.98 us -> none  [on_device(): density_in + cheb_coeffs[0] * cheb_mid.astype(jnp.float32)]
    slice x1 -> x0, local copies, waits for them, and re-layouts: 0.58 us -> none  [on_device(): cheb_coeffs[0] * cheb_mid.astype(jnp.float32)]
where the time goes in v2:
time: 48.3 us; the launch traced here: 48.2 us
  Pallas kernels  45 us (93%)
  local copies, waits for them, and re-layouts  1.87 us (4%)
  between operations  1.3 us (3%)
    pallas_call x1, Pallas kernels, on_device(): pl.pallas_call(kernel, name='two_steps', out_shape=results, in_specs=[in_...  35.9 us
    pallas_call x1, Pallas kernels, on_device(): pl.pallas_call(hand_over, name='hand_over', out_shape=results, in_specs=[...  9.07 us
    unnamed x6, local copies, waits for them, and re-layouts  1.87 us

profile of v2, /device:TPU:1, one launch (start us, length us, event | category | flops | bytes accessed | tf_op | source)
XLA Modules:
  0.0 48.2 jit_solution(13705372103729024785)
XLA Ops:
  1.3 35.9 %two_steps.1 = (bf16[1,1,1,2,128,128]{5,4,3,2,1,0:T(8,128)(2,1)S(1)}, bf16[1,1,1,2,128,128]{5,4,3,2,1,0:T(8,128)(2,1)S(1)}, f32[1,1,1,2,128,128]{5,4,3,2,1,0:T(8,128)S(1)}) custom-call(bf16[1,1,1,2,128,128]{5,4,3,2,1,0:T(8,128)(2,1)} %curr_hbm.1, bf16[1,1,1,2,128,128]{5,4,3,2,1,0:T(8,128)(2,1)} %prev_hbm.1, bf16[1,1,1,2,48,128,128]{6,5,4,3,2,1,0:T(8,128)(2,1)} %h_hbm.1, ...), custom_call_target="tpu_custom_call" | custom-call | tf_op jit(solution)/shard_map/two_steps/pallas_call | solution.py:348
  37.2 0.0 copy-start
  37.2 0.6 %copy-done = f32[1,1,1,2,128,128]{5,4,3,2,1,0:T(8,128)} copy-done((f32[1,1,1,2,128,128]{5,4,3,2,1,0:T(8,128)}, f32[1,1,1,2,128,128]{5,4,3,2,1,0:T(8,128)S(1)}, u32[]{:S(2)}) %copy-start) | copy-done | bytes 131096
  37.9 0.0 copy-start.1
  37.9 0.6 %copy-done.1 = bf16[1,1,1,2,128,128]{5,4,3,2,1,0:T(8,128)(2,1)} copy-done((bf16[1,1,1,2,128,128]{5,4,3,2,1,0:T(8,128)(2,1)}, bf16[1,1,1,2,128,128]{5,4,3,2,1,0:T(8,128)(2,1)S(1)}, u32[]{:S(2)}) %copy-start.1) | copy-done | bytes 65560
  38.5 0.0 copy-start.2
  38.5 0.6 %copy-done.2 = bf16[1,1,1,2,128,128]{5,4,3,2,1,0:T(8,128)(2,1)} copy-done((bf16[1,1,1,2,128,128]{5,4,3,2,1,0:T(8,128)(2,1)}, bf16[1,1,1,2,128,128]{5,4,3,2,1,0:T(8,128)(2,1)S(1)}, u32[]{:S(2)}) %copy-start.2) | copy-done | bytes 65560
  39.1 9.1 %hand_over.1 = (bf16[1,1,1,2,128,128]{5,4,3,2,1,0:T(8,128)(2,1)}, bf16[1,1,1,2,128,128]{5,4,3,2,1,0:T(8,128)(2,1)}, f32[1,1,1,2,128,128]{5,4,3,2,1,0:T(8,128)}) custom-call(bf16[1,1,1,2,128,128]{5,4,3,2,1,0:T(8,128)(2,1)} %copy-done.1, bf16[1,1,1,2,128,128]{5,4,3,2,1,0:T(8,128)(2,1)} %copy-done.2, f32[1,1,1,2,128,128]{5,4,3,2,1,0:T(8,128)} %copy-done), custom_call_target="tpu_custom_call" | custom-call | tf_op jit(solution)/shard_map/hand_over/pallas_call | solution.py:384
Async XLA Ops:
  37.2 0.6 %copy-start = (f32[1,1,1,2,128,128]{5,4,3,2,1,0:T(8,128)}, f32[1,1,1,2,128,128]{5,4,3,2,1,0:T(8,128)S(1)}, u32[]{:S(2)}) copy-start(f32[1,1,1,2,128,128]{5,4,3,2,1,0:T(8,128)S(1)} %get-tuple-element.8.refs_2_) | copy-start | bytes 393220
  37.9 0.6 %copy-start.1 = (bf16[1,1,1,2,128,128]{5,4,3,2,1,0:T(8,128)(2,1)}, bf16[1,1,1,2,128,128]{5,4,3,2,1,0:T(8,128)(2,1)S(1)}, u32[]{:S(2)}) copy-start(bf16[1,1,1,2,128,128]{5,4,3,2,1,0:T(8,128)(2,1)S(1)} %get-tuple-element.6.refs_0_) | copy-start | bytes 196612
  38.5 0.6 %copy-start.2 = (bf16[1,1,1,2,128,128]{5,4,3,2,1,0:T(8,128)(2,1)}, bf16[1,1,1,2,128,128]{5,4,3,2,1,0:T(8,128)(2,1)S(1)}, u32[]{:S(2)}) copy-start(bf16[1,1,1,2,128,128]{5,4,3,2,1,0:T(8,128)(2,1)S(1)} %get-tuple-element.7.refs_1_) | copy-start | bytes 196612

commit v3 on v2

--- a/solution.py
+++ b/solution.py
@@ -385,10 +385,10 @@
             hand_over,
             name="hand_over",
             out_shape=results,
-            in_specs=[pl.BlockSpec(memory_space=pl.ANY)] * 3,
+            in_specs=[in_vmem] * 3,
             out_specs=(in_hbm,) * 3,
             scratch_shapes=[pltpu.SemaphoreType.DMA((3,))],
-        )(*made)
+        )(*(pltpu.with_memory_space_constraint(array, pltpu.VMEM) for array in made))
     )
 
 

time: 48.3 us -> 38.1 us (0.79)
  Pallas kernels: 45 us -> 36.7 us
  local copies, waits for them, and re-layouts: 1.87 us -> 0 us
    pallas_call x1, Pallas kernels: 9.07 us -> 0.73 us  [on_device(): pl.pallas_call(hand_over, name='hand_over', out_shape=results, in_specs=[...]
    unnamed x6 -> x0, local copies, waits for them, and re-layouts: 1.87 us -> none
where the time goes in v3:
time: 38.1 us; the launch traced here: 37.9 us
  Pallas kernels  36.7 us (96%)
  between operations  1.29 us (3%)
    pallas_call x1, Pallas kernels, on_device(): pl.pallas_call(kernel, name='two_steps', out_shape=results, in_specs=[in_...  35.9 us

profile of v3, /device:TPU:1, one launch (start us, length us, event | category | flops | bytes accessed | tf_op | source)
XLA Modules:
  0.0 37.9 jit_solution(16948385266395201270)
XLA Ops:
  1.3 35.9 %two_steps.1 = (bf16[1,1,1,2,128,128]{5,4,3,2,1,0:T(8,128)(2,1)S(1)}, bf16[1,1,1,2,128,128]{5,4,3,2,1,0:T(8,128)(2,1)S(1)}, f32[1,1,1,2,128,128]{5,4,3,2,1,0:T(8,128)S(1)}) custom-call(bf16[1,1,1,2,128,128]{5,4,3,2,1,0:T(8,128)(2,1)} %curr_hbm.1, bf16[1,1,1,2,128,128]{5,4,3,2,1,0:T(8,128)(2,1)} %prev_hbm.1, bf16[1,1,1,2,48,128,128]{6,5,4,3,2,1,0:T(8,128)(2,1)} %h_hbm.1, ...), custom_call_target="tpu_custom_call" | custom-call | tf_op jit(solution)/shard_map/two_steps/pallas_call | solution.py:348
  37.2 0.7 %hand_over.1 = (bf16[1,1,1,2,128,128]{5,4,3,2,1,0:T(8,128)(2,1)}, bf16[1,1,1,2,128,128]{5,4,3,2,1,0:T(8,128)(2,1)}, f32[1,1,1,2,128,128]{5,4,3,2,1,0:T(8,128)}) custom-call(bf16[1,1,1,2,128,128]{5,4,3,2,1,0:T(8,128)(2,1)S(1)} %get-tuple-element.6.refs_0_, bf16[1,1,1,2,128,128]{5,4,3,2,1,0:T(8,128)(2,1)S(1)} %get-tuple-element.7.refs_1_, ...), custom_call_target="tpu_custom_call" | custom-call | tf_op jit(solution)/shard_map/hand_over/pallas_call | solution.py:384

commit v4 on v3

v4 whole, which is shorter than its diff:
```python
import functools

import jax
import jax.numpy as jnp
from jax import lax
from jax.experimental import pallas as pl
from jax.experimental.pallas import tpu as pltpu
from jax.sharding import PartitionSpec as P

MESH = pl.DeviceIdType.MESH
ROUNDS = 2

OWN, CROSS, PARTNER = 0, 1, 2
STAY, NEAR, FAR, AHEAD, BEHIND = 0, 1, 2, 3, 4
UP, DOWN, BOTH = 1, 2, 3
WAIT, SEND, ADD = 0, 1, 2

FIRST_SENDS = (
    ((0, 0, 0, 2), FAR, OWN, STAY),
    ((0, 0, 0, 1), NEAR, OWN, STAY),
    ((0, 0, 1, 2), FAR, CROSS, STAY),
    ((0, 0, 1, 1), NEAR, CROSS, STAY),
    ((0, 0, 1, 0), STAY, CROSS, STAY),
    ((0, 1, 0, 0), STAY, OWN, UP),
    ((0, 2, 0, 0), STAY, OWN, DOWN),
    ((0, 0, 2, 0), STAY, PARTNER, STAY),
)
SECOND_SENDS = (
    ((1, 1, 0, 0), STAY, OWN, BOTH),
    ((1, 0, 1, 1), NEAR, CROSS, STAY),
    ((1, 0, 0, 2), FAR, OWN, STAY),
    ((1, 0, 0, 1), NEAR, OWN, STAY),
    ((1, 0, 1, 0), STAY, CROSS, STAY),
    ((1, 0, 2, 0), STAY, PARTNER, STAY),
)
ORDER = (
    (WAIT, (0, 0, 2, 0)),
    (WAIT, (1, 0, 2, 0)),
    (WAIT, (0, 1, 0, 0)),
    (WAIT, (0, 2, 0, 0)),
    (
        SEND,
        (0, 1, 0, 0),
        (
            ((0, 1, 2, 0), STAY, PARTNER, STAY),
        ),
    ),
    (
        SEND,
        (0, 2, 0, 0),
        (
            ((0, 2, 2, 0), STAY, PARTNER, STAY),
        ),
    ),
    (WAIT, (0, 0, 1, 0)),
    (
        SEND,
        (0, 0, 1, 0),
        (
            ((0, 1, 1, 0), STAY, OWN, UP),
            ((0, 2, 1, 0), STAY, OWN, DOWN),
        ),
    ),
    (WAIT, (1, 1, 0, 0)),
    (
        SEND,
        (1, 1, 0, 0),
        (
            ((1, 1, 0, 2), FAR, OWN, STAY),
            ((1, 1, 0, 1), NEAR, OWN, STAY),
            ((1, 1, 1, 2), FAR, CROSS, STAY),
            ((1, 1, 1, 1), NEAR, CROSS, STAY),
            ((1, 1, 1, 0), STAY, CROSS, STAY),
            ((1, 1, 2, 0), STAY, PARTNER, STAY),
        ),
    ),
    (WAIT, (0, 1, 2, 0)),
    (WAIT, (0, 2, 2, 0)),
    (WAIT, (0, 0, 0, 2)),
    (
        SEND,
        (0, 0, 0, 2),
        (
            ((0, 1, 0, 2), STAY, OWN, UP),
            ((0, 2, 0, 2), STAY, OWN, DOWN),
            ((0, 0, 2, 2), STAY, PARTNER, STAY),
        ),
    ),
    (WAIT, (0, 0, 0, 1)),
    (
        SEND,
        (0, 0, 0, 1),
        (
            ((0, 1, 0, 1), STAY, OWN, UP),
            ((0, 2, 0, 1), STAY, OWN, DOWN),
            ((0, 0, 2, 1), STAY, PARTNER, STAY),
        ),
    ),
    (WAIT, (0, 0, 1, 1)),
    (
        SEND,
        (0, 0, 1, 1),
        (
            ((0, 1, 1, 1), STAY, OWN, UP),
            ((0, 2, 1, 1), STAY, OWN, DOWN),
        ),
    ),
    (WAIT, (1, 1, 2, 0)),
    (WAIT, (0, 0, 1, 2)),
    (
        SEND,
        (0, 0, 1, 2),
        (
            ((0, 1, 1, 2), STAY, OWN, UP),
            ((0, 2, 1, 2), STAY, OWN, DOWN),
        ),
    ),
    (ADD, (0, 0, 0)),
    (WAIT, (1, 0, 1, 1)),
    (
        SEND,
        (1, 0, 1, 1),
        (
            ((1, 0, 1, 2), AHEAD, OWN, STAY),
        ),
    ),
    (WAIT, (0, 0, 2, 2)),
    (ADD, (0, 0, 1)),
    (WAIT, (0, 0, 2, 1)),
    (WAIT, (1, 0, 1, 0)),
    (ADD, (0, 0, 2)),
    (WAIT, (0, 1, 1, 0)),
    (WAIT, (0, 2, 1, 0)),
    (WAIT, (1, 0, 0, 2)),
    (
        SEND,
        (1, 0, 0, 2),
        (
            ((1, 0, 2, 2), STAY, PARTNER, STAY),
        ),
    ),
    (WAIT, (1, 0, 0, 1)),
    (
        SEND,
        (1, 0, 0, 1),
        (
            ((1, 0, 2, 1), STAY, PARTNER, STAY),
        ),
    ),
    (WAIT, (1, 1, 1, 0)),
    (WAIT, (0, 1, 0, 2)),
    (WAIT, (0, 2, 0, 2)),
    (
        SEND,
        (0, 1, 0, 2),
        (
            ((0, 1, 2, 2), STAY, PARTNER, STAY),
        ),
    ),
    (
        SEND,
        (0, 2, 0, 2),
        (
            ((0, 2, 2, 2), STAY, PARTNER, STAY),
        ),
    ),
    (ADD, (1, 0, 0)),
    (WAIT, (1, 0, 2, 2)),
    (WAIT, (1, 0, 2, 1)),
    (WAIT, (0, 1, 0, 1)),
    (WAIT, (0, 2, 0, 1)),
    (
        SEND,
        (0, 1, 0, 1),
        (
            ((0, 1, 2, 1), STAY, PARTNER, STAY),
        ),
    ),
    (
        SEND,
        (0, 2, 0, 1),
        (
            ((0, 2, 2, 1), STAY, PARTNER, STAY),
        ),
    ),
    (WAIT, (1, 1, 0, 2)),
    (
        SEND,
        (1, 1, 0, 2),
        (
            ((1, 1, 2, 2), STAY, PARTNER, STAY),
        ),
    ),
    (WAIT, (1, 1, 0, 1)),
    (WAIT, (1, 0, 1, 2)),
    (
        SEND,
        (1, 1, 0, 1),
        (
            ((1, 1, 2, 1), STAY, PARTNER, STAY),
        ),
    ),
    (WAIT, (1, 1, 1, 1)),
    (WAIT, (0, 1, 2, 2)),
    (WAIT, (0, 2, 2, 2)),
    (ADD, (1, 0, 2)),
    (ADD, (0, 1, 0)),
    (ADD, (0, 2, 0)),
    (WAIT, (1, 1, 1, 2)),
    (ADD, (1, 1, 0)),
    (ADD, (1, 0, 1)),
    (WAIT, (0, 1, 2, 1)),
    (WAIT, (0, 2, 2, 1)),
    (WAIT, (1, 1, 2, 2)),
    (WAIT, (0, 1, 1, 1)),
    (WAIT, (0, 2, 1, 1)),
    (ADD, (1, 1, 1)),
    (WAIT, (1, 1, 2, 1)),
    (WAIT, (0, 1, 1, 2)),
    (WAIT, (0, 2, 1, 2)),
    (ADD, (0, 1, 2)),
    (ADD, (0, 2, 2)),
    (ADD, (1, 1, 2)),
    (ADD, (0, 1, 1)),
    (ADD, (0, 2, 1)),
)


def kernel(
    curr_hbm,
    prev_hbm,
    h_hbm,
    listed_hbm,
    counts_hbm,
    density_hbm,
    coeffs_hbm,
    mid_ref,
    next_ref,
    density_ref,
    first,
    second,
    blocks,
    prev,
    raw,
    total,
    place_rows,
    place,
    listed,
    counts,
    coeffs,
    local_sem,
    send_sem,
    first_sem,
    second_sem,
):
    extent_x, extent_y, extent_z = (lax.axis_size(a) for a in ("gx", "gy", "gz"))
    x, y, z = (lax.axis_index(a) for a in ("gx", "gy", "gz"))
    slots, coupled, size = h_hbm.shape[3:6]
    side = 1 - 2 * (x % 2)
    lean = 1 - 2 * (y % 2)
    along_x = tuple((x + step * side + extent_x) % extent_x for step in (0, 1, -1, 2, -2))
    along_y = tuple((y + step * lean + extent_y) % extent_y for step in (0, -1, 1))
    along_z = tuple((z + step + extent_z) % extent_z for step in (0, 1, -1))
    inner = (z > 0) & (z < extent_z - 1)
    toward = jnp.where(z < extent_z // 2, 1, -1)

    def device(way):
        return along_x[way[0]], along_y[way[1]], along_z[way[2]]

    def single(way):
        return tuple(way[:2] + (step,) for step in ((UP, DOWN) if way[2] == BOTH else way[2:]))

    sends = FIRST_SENDS + SECOND_SENDS + sum((step[2] for step in ORDER if step[0] == SEND), ())
    ways = sorted({way for _, *rest in sends for way in single(tuple(rest))})
    back_x, back_z = (STAY, NEAR, FAR, BEHIND, AHEAD), (STAY, DOWN, UP)
    barrier = pltpu.get_barrier_semaphore()
    for way in ways:
        source = device((back_x[way[0]], way[1], back_z[way[2]]))
        pl.semaphore_signal(barrier, inc=1, device_id=source, device_id_type=MESH)

    load_counts = pltpu.make_async_copy(counts_hbm, counts, local_sem.at[0])
    load_raw = pltpu.make_async_copy(curr_hbm.at[0, 0, 0, 1], raw, local_sem.at[1])
    load_listed = pltpu.make_async_copy(listed_hbm, listed, local_sem.at[2])
    load_first = pltpu.make_async_copy(
        curr_hbm.at[0, 0, 0, 0], first.at[0, 0, OWN, 0], local_sem.at[3]
    )
    load_blocks = pltpu.make_async_copy(
        h_hbm.at[0, 0, 0], blocks.at[:, pl.ds(0, coupled)], local_sem.at[4]
    )
    load_prev = pltpu.make_async_copy(prev_hbm.at[0, 0, 0], prev, local_sem.at[5])
    load_density = pltpu.make_async_copy(density_hbm, density_ref, local_sem.at[6])
    load_coeffs = pltpu.make_async_copy(coeffs_hbm, coeffs, local_sem.at[7])
    for load in (
        load_counts,
        load_raw,
        load_listed,
        load_first,
        load_blocks,
        load_prev,
        load_density,
        load_coeffs,
    ):
        load.start()
    pl.semaphore_wait(barrier, len(ways))

    pending = []
    held = ((first, first_sem), (second, second_sem))

    def forward(step, block, sends, source=None):
        slot = block[0]
        ref, semaphores = held[slot]
        if source is None:
            source = ref.at[(step,) + block[1:]]
        when = inner if slot == 1 and block[1] == 0 else None
        for target, *rest in sends:
            at = (step,) + target[1:]
            for way in single(tuple(rest)):
                copy = pltpu.make_async_remote_copy(
                    src_ref=source,
                    dst_ref=ref.at[at],
                    send_sem=send_sem.at[len(pending)],
                    recv_sem=semaphores.at[at],
                    device_id=device(way),
                    device_id_type=MESH,
                )
                pending.append((copy, when))
                if when is None:
                    copy.start()
                else:
                    pl.when(when)(copy.start)

    def arrived(step, block):
        ref, semaphores = held[block[0]]
        at = (step,) + block[1:]
        copy = pltpu.make_async_remote_copy(
            src_ref=ref.at[at],
            dst_ref=ref.at[at],
            send_sem=send_sem.at[0],
            recv_sem=semaphores.at[at],
            device_id=device((STAY, PARTNER, STAY)),
            device_id_type=MESH,
        )
        if block[0] == 1 and block[1] == 0:
            pl.when(inner)(copy.wait_recv)
        else:
            copy.wait_recv()

    shift_x = (0, side, -side)
    shift_y = (0, -lean, lean)

    def add(step, slot, layer, column, start):
        shift_z = 0 if layer == 0 else toward if slot == 1 else 2 * layer - 3

        def multiply():
            rows = []
            for row in range(slots):
                parts = []
                for group in range(3):
                    offset = (shift_x[group] + 1) * 9 + (shift_y[column] + 1) * 3 + shift_z + 1
                    parts.append(blocks[row, place[row, offset * slots + slot]])
                rows.append(jnp.concatenate(parts, axis=1))
            product = jnp.dot(
                jnp.concatenate(rows, axis=0),
                held[slot][0][step, layer, column].reshape(3 * size, -1),
                preferred_element_type=jnp.float32,
            )
            total[...] = product if start else total[...] + product

        if slot == 1 and layer == 0:
            pl.when(inner)(multiply)
        else:
            multiply()

    def apply(step, before_first):
        started = False
        for kind, block, *rest in ORDER:
            if kind == WAIT:
                arrived(step, block)
            elif kind == SEND:
                own = curr_hbm.at[0, 0, 0, 0] if step == 0 and block == (0, 0, OWN, 0) else None
                forward(step, block, rest[0], own)
            else:
                if not started:
                    before_first()
                add(step, *block, not started)
                started = True

    forward(0, (0, 0, OWN, 0), FIRST_SENDS, curr_hbm.at[0, 0, 0, 0])
    load_counts.wait()
    load_raw.wait()
    live = counts[0, 0, 0] > 1
    second[0, 0, OWN, 0] = jnp.where(live, raw[...].astype(jnp.float32), 0.0).astype(raw.dtype)
    forward(0, (1, 0, OWN, 0), SECOND_SENDS)

    load_listed.wait()
    blocks[:, pl.ds(coupled, 1)] = jnp.zeros((slots, 1, size, size), blocks.dtype)
    lanes = lax.broadcasted_iota(jnp.int32, (1, place_rows.shape[1]), 1)
    for row in range(slots):
        found = jnp.full(lanes.shape, coupled, jnp.int32)
        for item in range(coupled):
            found = jnp.where(lanes == listed[0, 0, 0, row, item], item, found)
        place_rows[pl.ds(row, 1), :] = found
    load_place = pltpu.make_async_copy(place_rows, place, local_sem.at[8])
    load_place.start()
    load_first.wait()
    load_prev.wait()

    def before_first():
        load_place.wait()
        load_blocks.wait()

    apply(0, before_first)

    def product_less(row, before):
        value = 2.0 * total[pl.ds(row * size, size), :] - before.astype(jnp.float32)
        if row:
            value = jnp.where(live, value, 0.0)
        return value.astype(raw.dtype)

    mid = product_less(0, prev[0])
    first[1, 0, OWN, 0] = mid
    forward(1, (0, 0, OWN, 0), FIRST_SENDS)
    mid_ref[0, 0, 0, 0] = mid
    mid = product_less(1, prev[1])
    second[1, 0, OWN, 0] = mid
    forward(1, (1, 0, OWN, 0), SECOND_SENDS)
    mid_ref[0, 0, 0, 1] = mid

    load_density.wait()
    load_coeffs.wait()
    density_ref[...] += coeffs[0] * mid_ref[...].astype(jnp.float32)
    apply(1, lambda: None)
    for row in range(slots):
        value = product_less(row, held[row][0][0, 0, OWN, 0])
        next_ref[0, 0, 0, row] = value
        density_ref[0, 0, 0, row] += coeffs[1] * value.astype(jnp.float32)
    for copy, when in pending:
        if when is None:
            copy.wait_send()
        else:
            pl.when(when)(copy.wait_send)


def hand_over(*refs):
    count = len(refs) // 2
    sources, targets, semaphores = refs[:count], refs[count : 2 * count], refs[-1]
    copies = [
        pltpu.make_async_copy(source, target, semaphores.at[index])
        for index, (source, target) in enumerate(zip(sources, targets))
    ]
    for copy in copies:
        copy.start()
    for copy in copies:
        copy.wait()


def on_device(
    h_blocks, neighbours, block_counts, cheb_prev_in, cheb_curr_in, density_in, cheb_coeffs
):
    slots, coupled, size = h_blocks.shape[3:6]
    field = cheb_curr_in.shape
    probes = field[5]
    kind = cheb_curr_in.dtype
    in_hbm = pl.BlockSpec(memory_space=pltpu.HBM)
    in_vmem = pl.BlockSpec(memory_space=pltpu.VMEM)
    kept = functools.partial(pltpu.with_memory_space_constraint, memory_space=pltpu.HBM)
    results = (
        jax.ShapeDtypeStruct(field, kind),
        jax.ShapeDtypeStruct(field, kind),
        jax.ShapeDtypeStruct(field, jnp.float32),
    )
    made = pl.pallas_call(
        kernel,
        name="two_steps",
        out_shape=results,
        in_specs=[in_hbm] * 7,
        out_specs=(in_vmem,) * 3,
        scratch_shapes=[
            pltpu.VMEM((ROUNDS, 3, 3, 3, size, probes), kind),
            pltpu.VMEM((ROUNDS, 2, 3, 3, size, probes), kind),
            pltpu.VMEM((slots, coupled + 1, size, size), h_blocks.dtype),
            pltpu.VMEM((slots, size, probes), kind),
            pltpu.VMEM((size, probes), kind),
            pltpu.VMEM((slots * size, probes), jnp.float32),
            pltpu.VMEM((8, 128), jnp.int32),
            pltpu.SMEM((8, 128), jnp.int32),
            pltpu.SMEM(neighbours.shape, jnp.int32),
            pltpu.SMEM(block_counts.shape, jnp.int32),
            pltpu.SMEM(cheb_coeffs.shape, jnp.float32),
            pltpu.SemaphoreType.DMA((9,)),
            pltpu.SemaphoreType.DMA((ROUNDS * 64,)),
            pltpu.SemaphoreType.DMA((ROUNDS, 3, 3, 3)),
            pltpu.SemaphoreType.DMA((ROUNDS, 2, 3, 3)),
        ],
        compiler_params=pltpu.CompilerParams(
            collective_id=0, has_side_effects=True, vmem_limit_bytes=32 * 2**20
        ),
    )(
        kept(cheb_curr_in),
        kept(cheb_prev_in),
        kept(h_blocks),
        kept(neighbours),
        block_counts,
        kept(density_in),
        kept(cheb_coeffs),
    )
    return tuple(
        pl.pallas_call(
            hand_over,
            name="hand_over",
            out_shape=results,
            in_specs=[in_vmem] * 3,
            out_specs=(in_hbm,) * 3,
            scratch_shapes=[pltpu.SemaphoreType.DMA((3,))],
        )(*(pltpu.with_memory_space_constraint(array, pltpu.VMEM) for array in made))
    )


def solution(mesh):
    placed = (
        P("gx", "gy", "gz", None, None, None, None),
        P("gx", "gy", "gz", None, None),
        P("gx", "gy", "gz"),
        P("gx", "gy", "gz", None, None, None),
        P("gx", "gy", "gz", None, None, None),
        P("gx", "gy", "gz", None, None, None),
        P(),
    )
    return jax.shard_map(
        on_device,
        mesh=mesh,
        in_specs=placed,
        out_specs=(
            P("gx", "gy", "gz", None, None, None),
            P("gx", "gy", "gz", None, None, None),
            P("gx", "gy", "gz", None, None, None),
        ),
        check_vma=False,
    )
```

time: 38.1 us -> 35.5 us (0.932)
  Pallas kernels: 36.7 us -> 34 us
    pallas_call x1, Pallas kernels: 35.9 us -> 33.3 us  [on_device(): pl.pallas_call(kernel, name='two_steps', out_shape=results, in_specs=[in_...]
where the time goes in v4:
time: 35.5 us; the launch traced here: 35.3 us
  Pallas kernels  34 us (96%)
  between operations  1.29 us (4%)
    pallas_call x1, Pallas kernels, on_device(): pl.pallas_call(kernel, name='two_steps', out_shape=results, in_specs=[in_...  33.3 us
    pallas_call x1, Pallas kernels, on_device(): pl.pallas_call(hand_over, name='hand_over', out_shape=results, in_specs=[...  0.73 us

profile of v4, /device:TPU:1, one launch (start us, length us, event | category | flops | bytes accessed | tf_op | source)
XLA Modules:
  0.0 35.3 jit_solution(13861664503965909801)
XLA Ops:
  1.3 33.3 %two_steps.1 = (bf16[1,1,1,2,128,128]{5,4,3,2,1,0:T(8,128)(2,1)S(1)}, bf16[1,1,1,2,128,128]{5,4,3,2,1,0:T(8,128)(2,1)S(1)}, f32[1,1,1,2,128,128]{5,4,3,2,1,0:T(8,128)S(1)}) custom-call(bf16[1,1,1,2,128,128]{5,4,3,2,1,0:T(8,128)(2,1)} %curr_hbm.1, bf16[1,1,1,2,128,128]{5,4,3,2,1,0:T(8,128)(2,1)} %prev_hbm.1, bf16[1,1,1,2,48,128,128]{6,5,4,3,2,1,0:T(8,128)(2,1)} %h_hbm.1, ...), custom_call_target="tpu_custom_call" | custom-call | tf_op jit(solution)/shard_map/two_steps/pallas_call | solution.py:472
  34.6 0.7 %hand_over.1 = (bf16[1,1,1,2,128,128]{5,4,3,2,1,0:T(8,128)(2,1)}, bf16[1,1,1,2,128,128]{5,4,3,2,1,0:T(8,128)(2,1)}, f32[1,1,1,2,128,128]{5,4,3,2,1,0:T(8,128)}) custom-call(bf16[1,1,1,2,128,128]{5,4,3,2,1,0:T(8,128)(2,1)S(1)} %get-tuple-element.6.refs_0_, bf16[1,1,1,2,128,128]{5,4,3,2,1,0:T(8,128)(2,1)S(1)} %get-tuple-element.7.refs_1_, ...), custom_call_target="tpu_custom_call" | custom-call | tf_op jit(solution)/shard_map/hand_over/pallas_call | solution.py:508

commit v5 on v4

--- a/solution.py
+++ b/solution.py
@@ -27,15 +27,23 @@
 )
 SECOND_SENDS = (
     ((1, 1, 0, 0), STAY, OWN, BOTH),
-    ((1, 0, 1, 1), NEAR, CROSS, STAY),
     ((1, 0, 0, 2), FAR, OWN, STAY),
     ((1, 0, 0, 1), NEAR, OWN, STAY),
+    ((1, 0, 2, 0), STAY, PARTNER, STAY),
+    ((1, 0, 1, 2), FAR, CROSS, STAY),
+    ((1, 0, 1, 1), NEAR, CROSS, STAY),
     ((1, 0, 1, 0), STAY, CROSS, STAY),
-    ((1, 0, 2, 0), STAY, PARTNER, STAY),
 )
 ORDER = (
     (WAIT, (0, 0, 2, 0)),
     (WAIT, (1, 0, 2, 0)),
+    (
+        SEND,
+        (1, 0, 2, 0),
+        (
+            ((1, 1, 2, 0), STAY, OWN, BOTH),
+        ),
+    ),
     (WAIT, (0, 1, 0, 0)),
     (WAIT, (0, 2, 0, 0)),
     (
@@ -71,9 +79,9 @@
             ((1, 1, 1, 2), FAR, CROSS, STAY),
             ((1, 1, 1, 1), NEAR, CROSS, STAY),
             ((1, 1, 1, 0), STAY, CROSS, STAY),
-            ((1, 1, 2, 0), STAY, PARTNER, STAY),
-        ),
-    ),
+        ),
+    ),
+    (ADD, (0, 0, 0)),
     (WAIT, (0, 1, 2, 0)),
     (WAIT, (0, 2, 2, 0)),
     (WAIT, (0, 0, 0, 2)),
@@ -81,8 +89,8 @@
         SEND,
         (0, 0, 0, 2),
         (
+            ((0, 2, 0, 2), STAY, OWN, DOWN),
             ((0, 1, 0, 2), STAY, OWN, UP),
-            ((0, 2, 0, 2), STAY, OWN, DOWN),
             ((0, 0, 2, 2), STAY, PARTNER, STAY),
         ),
     ),
@@ -105,7 +113,6 @@
             ((0, 2, 1, 1), STAY, OWN, DOWN),
         ),
     ),
-    (WAIT, (1, 1, 2, 0)),
     (WAIT, (0, 0, 1, 2)),
     (
         SEND,
@@ -115,39 +122,38 @@
             ((0, 2, 1, 2), STAY, OWN, DOWN),
         ),
     ),
-    (ADD, (0, 0, 0)),
-    (WAIT, (1, 0, 1, 1)),
-    (
-        SEND,
-        (1, 0, 1, 1),
-        (
-            ((1, 0, 1, 2), AHEAD, OWN, STAY),
-        ),
-    ),
+    (WAIT, (1, 1, 2, 0)),
     (WAIT, (0, 0, 2, 2)),
-    (ADD, (0, 0, 1)),
     (WAIT, (0, 0, 2, 1)),
     (WAIT, (1, 0, 1, 0)),
     (ADD, (0, 0, 2)),
+    (ADD, (0, 0, 1)),
+    (WAIT, (1, 0, 0, 2)),
+    (
+        SEND,
+        (1, 0, 0, 2),
+        (
+            ((1, 0, 2, 2), STAY, PARTNER, STAY),
+        ),
+    ),
+    (WAIT, (1, 0, 0, 1)),
+    (
+        SEND,
+        (1, 0, 0, 1),
+        (
+            ((1, 0, 2, 1), STAY, PARTNER, STAY),
+        ),
+    ),
+    (WAIT, (1, 0, 1, 1)),
     (WAIT, (0, 1, 1, 0)),
     (WAIT, (0, 2, 1, 0)),
-    (WAIT, (1, 0, 0, 2)),
-    (
-        SEND,
-        (1, 0, 0, 2),
-        (
-            ((1, 0, 2, 2), STAY, PARTNER, STAY),
-        ),
-    ),
-    (WAIT, (1, 0, 0, 1)),
-    (
-        SEND,
-        (1, 0, 0, 1),
-        (
-            ((1, 0, 2, 1), STAY, PARTNER, STAY),
-        ),
-    ),
+    (WAIT, (1, 0, 1, 2)),
+    (ADD, (0, 1, 0)),
+    (ADD, (0, 2, 0)),
+    (WAIT, (1, 0, 2, 2)),
     (WAIT, (1, 1, 1, 0)),
+    (ADD, (1, 0, 0)),
+    (WAIT, (1, 0, 2, 1)),
     (WAIT, (0, 1, 0, 2)),
     (WAIT, (0, 2, 0, 2)),
     (
@@ -164,9 +170,17 @@
             ((0, 2, 2, 2), STAY, PARTNER, STAY),
         ),
     ),
-    (ADD, (1, 0, 0)),
-    (WAIT, (1, 0, 2, 2)),
-    (WAIT, (1, 0, 2, 1)),
+    (ADD, (1, 0, 2)),
+    (ADD, (1, 1, 0)),
+    (ADD, (1, 0, 1)),
+    (WAIT, (1, 1, 0, 1)),
+    (
+        SEND,
+        (1, 1, 0, 1),
+        (
+            ((1, 1, 2, 1), STAY, PARTNER, STAY),
+        ),
+    ),
     (WAIT, (0, 1, 0, 1)),
     (WAIT, (0, 2, 0, 1)),
     (
@@ -183,6 +197,7 @@
             ((0, 2, 2, 1), STAY, PARTNER, STAY),
         ),
     ),
+    (WAIT, (0, 2, 1, 1)),
     (WAIT, (1, 1, 0, 2)),
     (
         SEND,
@@ -191,37 +206,22 @@
             ((1, 1, 2, 2), STAY, PARTNER, STAY),
         ),
     ),
-    (WAIT, (1, 1, 0, 1)),
-    (WAIT, (1, 0, 1, 2)),
-    (
-        SEND,
-        (1, 1, 0, 1),
-        (
-            ((1, 1, 2, 1), STAY, PARTNER, STAY),
-        ),
-    ),
-    (WAIT, (1, 1, 1, 1)),
     (WAIT, (0, 1, 2, 2)),
     (WAIT, (0, 2, 2, 2)),
-    (ADD, (1, 0, 2)),
-    (ADD, (0, 1, 0)),
-    (ADD, (0, 2, 0)),
-    (WAIT, (1, 1, 1, 2)),
-    (ADD, (1, 1, 0)),
-    (ADD, (1, 0, 1)),
+    (WAIT, (0, 1, 1, 1)),
+    (WAIT, (1, 1, 1, 1)),
     (WAIT, (0, 1, 2, 1)),
     (WAIT, (0, 2, 2, 1)),
-    (WAIT, (1, 1, 2, 2)),
-    (WAIT, (0, 1, 1, 1)),
-    (WAIT, (0, 2, 1, 1)),
-    (ADD, (1, 1, 1)),
-    (WAIT, (1, 1, 2, 1)),
+    (WAIT, (1, 1, 1, 2)),
     (WAIT, (0, 1, 1, 2)),
     (WAIT, (0, 2, 1, 2)),
+    (ADD, (0, 1, 1)),
     (ADD, (0, 1, 2)),
     (ADD, (0, 2, 2)),
+    (WAIT, (1, 1, 2, 2)),
+    (WAIT, (1, 1, 2, 1)),
     (ADD, (1, 1, 2)),
-    (ADD, (0, 1, 1)),
+    (ADD, (1, 1, 1)),
     (ADD, (0, 2, 1)),
 )
 
@@ -231,7 +231,7 @@
     prev_hbm,
     h_hbm,
     listed_hbm,
-    counts_hbm,
+    counts,
     density_hbm,
     coeffs_hbm,
     mid_ref,
@@ -246,7 +246,6 @@
     place_rows,
     place,
     listed,
-    counts,
     coeffs,
     local_sem,
     send_sem,
@@ -278,11 +277,10 @@
         source = device((back_x[way[0]], way[1], back_z[way[2]]))
         pl.semaphore_signal(barrier, inc=1, device_id=source, device_id_type=MESH)
 
-    load_counts = pltpu.make_async_copy(counts_hbm, counts, local_sem.at[0])
     load_raw = pltpu.make_async_copy(curr_hbm.at[0, 0, 0, 1], raw, local_sem.at[1])
     load_listed = pltpu.make_async_copy(listed_hbm, listed, local_sem.at[2])
     load_first = pltpu.make_async_copy(
-        curr_hbm.at[0, 0, 0, 0], first.at[0, 0, OWN, 0], local_sem.at[3]
+        curr_hbm.at[0, 0, 0, 0], first.at[0, 0, 0, OWN], local_sem.at[3]
     )
     load_blocks = pltpu.make_async_copy(
         h_hbm.at[0, 0, 0], blocks.at[:, pl.ds(0, coupled)], local_sem.at[4]
@@ -291,7 +289,6 @@
     load_density = pltpu.make_async_copy(density_hbm, density_ref, local_sem.at[6])
     load_coeffs = pltpu.make_async_copy(coeffs_hbm, coeffs, local_sem.at[7])
     for load in (
-        load_counts,
         load_raw,
         load_listed,
         load_first,
@@ -310,28 +307,36 @@
         slot = block[0]
         ref, semaphores = held[slot]
         if source is None:
-            source = ref.at[(step,) + block[1:]]
+            source = ref.at[step, block[1], block[3], block[2]]
         when = inner if slot == 1 and block[1] == 0 else None
+        copies = []
         for target, *rest in sends:
-            at = (step,) + target[1:]
+            at = (step, target[1], target[3], target[2])
             for way in single(tuple(rest)):
-                copy = pltpu.make_async_remote_copy(
-                    src_ref=source,
-                    dst_ref=ref.at[at],
-                    send_sem=send_sem.at[len(pending)],
-                    recv_sem=semaphores.at[at],
-                    device_id=device(way),
-                    device_id_type=MESH,
+                copies.append(
+                    pltpu.make_async_remote_copy(
+                        src_ref=source,
+                        dst_ref=ref.at[at],
+                        send_sem=send_sem.at[len(pending)],
+                        recv_sem=semaphores.at[at],
+                        device_id=device(way),
+                        device_id_type=MESH,
+                    )
                 )
-                pending.append((copy, when))
-                if when is None:
-                    copy.start()
-                else:
-                    pl.when(when)(copy.start)
+                pending.append((copies[-1], when))
+
+        def start():
+            for copy in copies:
+                copy.start()
+
+        if when is None:
+            start()
+        else:
+            pl.when(when)(start)
 
     def arrived(step, block):
         ref, semaphores = held[block[0]]
-        at = (step,) + block[1:]
+        at = (step, block[1], block[3], block[2])
         copy = pltpu.make_async_remote_copy(
             src_ref=ref.at[at],
             dst_ref=ref.at[at],
@@ -348,20 +353,20 @@
     shift_x = (0, side, -side)
     shift_y = (0, -lean, lean)
 
-    def add(step, slot, layer, column, start):
+    def add(step, slot, layer, group, start):
         shift_z = 0 if layer == 0 else toward if slot == 1 else 2 * layer - 3
 
         def multiply():
             rows = []
             for row in range(slots):
                 parts = []
-                for group in range(3):
+                for column in range(3):
                     offset = (shift_x[group] + 1) * 9 + (shift_y[column] + 1) * 3 + shift_z + 1
                     parts.append(blocks[row, place[row, offset * slots + slot]])
                 rows.append(jnp.concatenate(parts, axis=1))
             product = jnp.dot(
                 jnp.concatenate(rows, axis=0),
-                held[slot][0][step, layer, column].reshape(3 * size, -1),
+                held[slot][0][step, layer, group].reshape(3 * size, -1),
                 preferred_element_type=jnp.float32,
             )
             total[...] = product if start else total[...] + product
@@ -386,10 +391,9 @@
                 started = True
 
     forward(0, (0, 0, OWN, 0), FIRST_SENDS, curr_hbm.at[0, 0, 0, 0])
-    load_counts.wait()
     load_raw.wait()
     live = counts[0, 0, 0] > 1
-    second[0, 0, OWN, 0] = jnp.where(live, raw[...].astype(jnp.float32), 0.0).astype(raw.dtype)
+    second[0, 0, 0, OWN] = jnp.where(live, raw[...].astype(jnp.float32), 0.0).astype(raw.dtype)
     forward(0, (1, 0, OWN, 0), SECOND_SENDS)
 
     load_listed.wait()
@@ -418,11 +422,11 @@
         return value.astype(raw.dtype)
 
     mid = product_less(0, prev[0])
-    first[1, 0, OWN, 0] = mid
+    first[1, 0, 0, OWN] = mid
     forward(1, (0, 0, OWN, 0), FIRST_SENDS)
     mid_ref[0, 0, 0, 0] = mid
     mid = product_less(1, prev[1])
-    second[1, 0, OWN, 0] = mid
+    second[1, 0, 0, OWN] = mid
     forward(1, (1, 0, OWN, 0), SECOND_SENDS)
     mid_ref[0, 0, 0, 1] = mid
 
@@ -431,14 +435,18 @@
     density_ref[...] += coeffs[0] * mid_ref[...].astype(jnp.float32)
     apply(1, lambda: None)
     for row in range(slots):
-        value = product_less(row, held[row][0][0, 0, OWN, 0])
+        value = product_less(row, held[row][0][0, 0, 0, OWN])
         next_ref[0, 0, 0, row] = value
         density_ref[0, 0, 0, row] += coeffs[1] * value.astype(jnp.float32)
     for copy, when in pending:
         if when is None:
             copy.wait_send()
-        else:
-            pl.when(when)(copy.wait_send)
+
+    @pl.when(inner)
+    def _():
+        for copy, when in pending:
+            if when is not None:
+                copy.wait_send()
 
 
 def hand_over(*refs):
@@ -462,6 +470,7 @@
     probes = field[5]
     kind = cheb_curr_in.dtype
     in_hbm = pl.BlockSpec(memory_space=pltpu.HBM)
+    in_smem = pl.BlockSpec(memory_space=pltpu.SMEM)
     in_vmem = pl.BlockSpec(memory_space=pltpu.VMEM)
     kept = functools.partial(pltpu.with_memory_space_constraint, memory_space=pltpu.HBM)
     results = (
@@ -473,7 +482,7 @@
         kernel,
         name="two_steps",
         out_shape=results,
-        in_specs=[in_hbm] * 7,
+        in_specs=[in_hbm] * 4 + [in_smem] + [in_hbm] * 2,
         out_specs=(in_vmem,) * 3,
         scratch_shapes=[
             pltpu.VMEM((ROUNDS, 3, 3, 3, size, probes), kind),
@@ -485,7 +494,6 @@
             pltpu.VMEM((8, 128), jnp.int32),
             pltpu.SMEM((8, 128), jnp.int32),
             pltpu.SMEM(neighbours.shape, jnp.int32),
-            pltpu.SMEM(block_counts.shape, jnp.int32),
             pltpu.SMEM(cheb_coeffs.shape, jnp.float32),
             pltpu.SemaphoreType.DMA((9,)),
             pltpu.SemaphoreType.DMA((ROUNDS * 64,)),

time: 35.5 us -> 35 us (0.986)
  Pallas kernels: 34 us -> 33.6 us
    pallas_call x1, Pallas kernels: 33.3 us -> 32.8 us  [on_device(): pl.pallas_call(kernel, name='two_steps', out_shape=results, in_specs=[in_...]
where the time goes in v5:
time: 35 us; the launch traced here: 34.8 us
  Pallas kernels  33.6 us (96%)
  between operations  1.29 us (4%)
    pallas_call x1, Pallas kernels, on_device(): pl.pallas_call(kernel, name='two_steps', out_shape=results, in_specs=[in_...  32.8 us
    pallas_call x1, Pallas kernels, on_device(): pl.pallas_call(hand_over, name='hand_over', out_shape=results, in_specs=[...  0.73 us

profile of v5, /device:TPU:1, one launch (start us, length us, event | category | flops | bytes accessed | tf_op | source)
XLA Modules:
  0.0 34.8 jit_solution(12445475492371851040)
XLA Ops:
  1.3 32.8 %two_steps.1 = (bf16[1,1,1,2,128,128]{5,4,3,2,1,0:T(8,128)(2,1)S(1)}, bf16[1,1,1,2,128,128]{5,4,3,2,1,0:T(8,128)(2,1)S(1)}, f32[1,1,1,2,128,128]{5,4,3,2,1,0:T(8,128)S(1)}) custom-call(bf16[1,1,1,2,128,128]{5,4,3,2,1,0:T(8,128)(2,1)} %curr_hbm.1, bf16[1,1,1,2,128,128]{5,4,3,2,1,0:T(8,128)(2,1)} %prev_hbm.1, bf16[1,1,1,2,48,128,128]{6,5,4,3,2,1,0:T(8,128)(2,1)} %h_hbm.1, ...), custom_call_target="tpu_custom_call" | custom-call | tf_op jit(solution)/shard_map/two_steps/pallas_call | solution.py:481
  34.1 0.7 %hand_over.1 = (bf16[1,1,1,2,128,128]{5,4,3,2,1,0:T(8,128)(2,1)}, bf16[1,1,1,2,128,128]{5,4,3,2,1,0:T(8,128)(2,1)}, f32[1,1,1,2,128,128]{5,4,3,2,1,0:T(8,128)}) custom-call(bf16[1,1,1,2,128,128]{5,4,3,2,1,0:T(8,128)(2,1)S(1)} %get-tuple-element.6.refs_0_, bf16[1,1,1,2,128,128]{5,4,3,2,1,0:T(8,128)(2,1)S(1)} %get-tuple-element.7.refs_1_, ...), custom_call_target="tpu_custom_call" | custom-call | tf_op jit(solution)/shard_map/hand_over/pallas_call | solution.py:516

commit v6 on v5

--- a/solution.py
+++ b/solution.py
@@ -273,7 +273,7 @@
     ways = sorted({way for _, *rest in sends for way in single(tuple(rest))})
     back_x, back_z = (STAY, NEAR, FAR, BEHIND, AHEAD), (STAY, DOWN, UP)
     barrier = pltpu.get_barrier_semaphore()
-    for way in ways:
+    for way in sorted(ways, key=lambda way: -sum(step != STAY for step in way)):
         source = device((back_x[way[0]], way[1], back_z[way[2]]))
         pl.semaphore_signal(barrier, inc=1, device_id=source, device_id_type=MESH)
 

time: 35 us -> 35 us (level)
  no operation moved by 1% of the time
where the time goes in v6:
time: 35 us; the launch traced here: 34.9 us
  Pallas kernels  33.6 us (96%)
  between operations  1.29 us (4%)
    pallas_call x1, Pallas kernels, on_device(): pl.pallas_call(kernel, name='two_steps', out_shape=results, in_specs=[in_...  32.8 us
    pallas_call x1, Pallas kernels, on_device(): pl.pallas_call(hand_over, name='hand_over', out_shape=results, in_specs=[...  0.73 us

profile of v6, /device:TPU:1, one launch (start us, length us, event | category | flops | bytes accessed | tf_op | source)
XLA Modules:
  0.0 34.9 jit_solution(11218882778233669192)
XLA Ops:
  1.3 32.8 %two_steps.1 = (bf16[1,1,1,2,128,128]{5,4,3,2,1,0:T(8,128)(2,1)S(1)}, bf16[1,1,1,2,128,128]{5,4,3,2,1,0:T(8,128)(2,1)S(1)}, f32[1,1,1,2,128,128]{5,4,3,2,1,0:T(8,128)S(1)}) custom-call(bf16[1,1,1,2,128,128]{5,4,3,2,1,0:T(8,128)(2,1)} %curr_hbm.1, bf16[1,1,1,2,128,128]{5,4,3,2,1,0:T(8,128)(2,1)} %prev_hbm.1, bf16[1,1,1,2,48,128,128]{6,5,4,3,2,1,0:T(8,128)(2,1)} %h_hbm.1, ...), custom_call_target="tpu_custom_call" | custom-call | tf_op jit(solution)/shard_map/two_steps/pallas_call | solution.py:481
  34.1 0.7 %hand_over.1 = (bf16[1,1,1,2,128,128]{5,4,3,2,1,0:T(8,128)(2,1)}, bf16[1,1,1,2,128,128]{5,4,3,2,1,0:T(8,128)(2,1)}, f32[1,1,1,2,128,128]{5,4,3,2,1,0:T(8,128)}) custom-call(bf16[1,1,1,2,128,128]{5,4,3,2,1,0:T(8,128)(2,1)S(1)} %get-tuple-element.6.refs_0_, bf16[1,1,1,2,128,128]{5,4,3,2,1,0:T(8,128)(2,1)S(1)} %get-tuple-element.7.refs_1_, ...), custom_call_target="tpu_custom_call" | custom-call | tf_op jit(solution)/shard_map/hand_over/pallas_call | solution.py:516

commit v7 on v6

--- a/solution.py
+++ b/solution.py
@@ -29,21 +29,14 @@
     ((1, 1, 0, 0), STAY, OWN, BOTH),
     ((1, 0, 0, 2), FAR, OWN, STAY),
     ((1, 0, 0, 1), NEAR, OWN, STAY),
-    ((1, 0, 2, 0), STAY, PARTNER, STAY),
     ((1, 0, 1, 2), FAR, CROSS, STAY),
     ((1, 0, 1, 1), NEAR, CROSS, STAY),
     ((1, 0, 1, 0), STAY, CROSS, STAY),
+    ((1, 0, 2, 0), STAY, PARTNER, STAY),
 )
 ORDER = (
     (WAIT, (0, 0, 2, 0)),
     (WAIT, (1, 0, 2, 0)),
-    (
-        SEND,
-        (1, 0, 2, 0),
-        (
-            ((1, 1, 2, 0), STAY, OWN, BOTH),
-        ),
-    ),
     (WAIT, (0, 1, 0, 0)),
     (WAIT, (0, 2, 0, 0)),
     (
@@ -79,6 +72,7 @@
             ((1, 1, 1, 2), FAR, CROSS, STAY),
             ((1, 1, 1, 1), NEAR, CROSS, STAY),
             ((1, 1, 1, 0), STAY, CROSS, STAY),
+            ((1, 1, 2, 0), STAY, PARTNER, STAY),
         ),
     ),
     (ADD, (0, 0, 0)),
@@ -89,8 +83,8 @@
         SEND,
         (0, 0, 0, 2),
         (
+            ((0, 1, 0, 2), STAY, OWN, UP),
             ((0, 2, 0, 2), STAY, OWN, DOWN),
-            ((0, 1, 0, 2), STAY, OWN, UP),
             ((0, 0, 2, 2), STAY, PARTNER, STAY),
         ),
     ),
@@ -128,6 +122,7 @@
     (WAIT, (1, 0, 1, 0)),
     (ADD, (0, 0, 2)),
     (ADD, (0, 0, 1)),
+    (ADD, (1, 0, 0)),
     (WAIT, (1, 0, 0, 2)),
     (
         SEND,
@@ -152,7 +147,6 @@
     (ADD, (0, 2, 0)),
     (WAIT, (1, 0, 2, 2)),
     (WAIT, (1, 1, 1, 0)),
-    (ADD, (1, 0, 0)),
     (WAIT, (1, 0, 2, 1)),
     (WAIT, (0, 1, 0, 2)),
     (WAIT, (0, 2, 0, 2)),
@@ -216,13 +210,13 @@
     (WAIT, (0, 1, 1, 2)),
     (WAIT, (0, 2, 1, 2)),
     (ADD, (0, 1, 1)),
+    (ADD, (0, 2, 1)),
     (ADD, (0, 1, 2)),
     (ADD, (0, 2, 2)),
     (WAIT, (1, 1, 2, 2)),
     (WAIT, (1, 1, 2, 1)),
     (ADD, (1, 1, 2)),
     (ADD, (1, 1, 1)),
-    (ADD, (0, 2, 1)),
 )
 
 

time: 35 us -> 34.9 us (level)
  no operation moved by 1% of the time
where the time goes in v7:
time: 34.9 us; the launch traced here: 34.8 us
  Pallas kernels  33.5 us (96%)
  between operations  1.29 us (4%)
    pallas_call x1, Pallas kernels, on_device(): pl.pallas_call(kernel, name='two_steps', out_shape=results, in_specs=[in_...  32.8 us
    pallas_call x1, Pallas kernels, on_device(): pl.pallas_call(hand_over, name='hand_over', out_shape=results, in_specs=[...  0.73 us

profile of v7, /device:TPU:1, one launch (start us, length us, event | category | flops | bytes accessed | tf_op | source)
XLA Modules:
  0.0 34.8 jit_solution(14800511755920456991)
XLA Ops:
  1.3 32.8 %two_steps.1 = (bf16[1,1,1,2,128,128]{5,4,3,2,1,0:T(8,128)(2,1)S(1)}, bf16[1,1,1,2,128,128]{5,4,3,2,1,0:T(8,128)(2,1)S(1)}, f32[1,1,1,2,128,128]{5,4,3,2,1,0:T(8,128)S(1)}) custom-call(bf16[1,1,1,2,128,128]{5,4,3,2,1,0:T(8,128)(2,1)} %curr_hbm.1, bf16[1,1,1,2,128,128]{5,4,3,2,1,0:T(8,128)(2,1)} %prev_hbm.1, bf16[1,1,1,2,48,128,128]{6,5,4,3,2,1,0:T(8,128)(2,1)} %h_hbm.1, ...), custom_call_target="tpu_custom_call" | custom-call | tf_op jit(solution)/shard_map/two_steps/pallas_call | solution.py:475
  34.1 0.7 %hand_over.1 = (bf16[1,1,1,2,128,128]{5,4,3,2,1,0:T(8,128)(2,1)}, bf16[1,1,1,2,128,128]{5,4,3,2,1,0:T(8,128)(2,1)}, f32[1,1,1,2,128,128]{5,4,3,2,1,0:T(8,128)}) custom-call(bf16[1,1,1,2,128,128]{5,4,3,2,1,0:T(8,128)(2,1)S(1)} %get-tuple-element.6.refs_0_, bf16[1,1,1,2,128,128]{5,4,3,2,1,0:T(8,128)(2,1)S(1)} %get-tuple-element.7.refs_1_, ...), custom_call_target="tpu_custom_call" | custom-call | tf_op jit(solution)/shard_map/hand_over/pallas_call | solution.py:510
